TPU v7x, 256 devices: a whole 4x4x8 slice. The times are simulated.
256 devices in a mesh: section: 16 (over z, core), dp: 16 (over y, x).
Axes of the slice: x: 4, y: 4, z: 8, core: 2. Of those that a mesh axis runs over, the one named last changes fastest.
Arguments:
- master: float32 [256, 262144], P('section', 'dp'), may hold values from -6 to 6
- momentum: float32 [256, 262144], P('section', 'dp'), may hold values from -0.6 to 0.6
- variance: float32 [256, 262144], P('section', 'dp'), may hold values from 0.001 to 0.1
- grads: float32 [65536, 1024], P(('section', 'dp')), may hold values from -6 to 6
- counts: int32 [256], replicated, may hold values from 131072 to 262144
- old_layers: int32 [256], replicated, may hold values from 0 to 255, as said below
- new_layers: int32 [256], replicated, may hold values from 0 to 255, as said below
Outputs:
- new_master: float32 [65536, 1024], P(('section', 'dp'))
- new_momentum: float32 [65536, 1024], P(('section', 'dp'))
- new_variance: float32 [65536, 1024], P(('section', 'dp'))
- params: bfloat16 [65536, 1024], P(('section', 'dp'))
Inputs may be any that keep to these rules, and one draw needn't show every extreme that they name: `old_layers`: a permutation of the layer ids. `new_layers`: a permutation of the layer ids; the 16 rows of each new section s (rows s * 16 to s * 16 + 15) hold exactly one layer from the rows of each old section j (rows j * 16 to j * 16 + 15 of old_layers), and that layer sits at row s * 16 + j.
All inputs are finite; a program needn't handle non-finite values.
Results may differ from a plain program's by a relative error of at most 0.001.
Values sent between devices are 32-bit elements; how exact they have to be, the bound alone decides.
No kernel may reach another device: no remote copies, remote signals or barrier semaphores. Data moves between devices by JAX's collectives and lax.ppermute only.
A program may use at most 64 MiB of HBM per device.

v0:
```python
import jax
import jax.numpy as jnp
from jax import lax
from jax.sharding import PartitionSpec as P

STEP = 1000


def locate(order, layer_ids):
    return jnp.sum(jnp.where(order[None, :] == layer_ids[:, None], layer_ids[None, :], 0), axis=1)


def adamw(weight, first, second, grad, limit, column):
    live = column[None, :] < limit[:, None]
    first = 0.9 * first + 0.1 * grad
    second = 0.95 * second + 0.05 * grad * grad
    step_size = first / (1.0 - 0.9**STEP) / (jnp.sqrt(second / (1.0 - 0.95**STEP)) + 1e-08)
    weight = weight - 0.01 * (step_size + 0.1 * weight)
    zero = jnp.float32(0.0)
    return (
        jnp.where(live, weight, zero),
        jnp.where(live, first, zero),
        jnp.where(live, second, zero),
    )


def on_device(master, momentum, variance, grads, counts, old_layers, new_layers):
    sections = lax.axis_size("section")
    ranks = lax.axis_size("dp")
    slots = master.shape[0]
    block = master.shape[1]
    width = block * ranks
    mine = slots // ranks
    total = old_layers.shape[0]
    here = lax.axis_index("section")
    rank = lax.axis_index("dp")
    layer_ids = jnp.arange(total, dtype=jnp.int32)
    old_row = locate(old_layers, layer_ids)
    new_row = locate(new_layers, layer_ids)
    held = lax.dynamic_slice_in_dim(old_layers, here * slots, slots)
    target = new_row[held] // slots
    section_ids = jnp.arange(sections, dtype=jnp.int32)
    slot_ids = jnp.arange(slots, dtype=jnp.int32)
    picks = jnp.sum(
        jnp.where(target[None, :] == section_ids[:, None], slot_ids[None, :], 0), axis=1
    )
    outgoing = (master[picks], momentum[picks], variance[picks])
    placed = lax.dynamic_slice_in_dim(new_layers, here * slots, slots)
    anchor = old_row[placed] // slots
    grad = grads.reshape(mine, width)
    full_columns = jnp.arange(width, dtype=jnp.int32)
    mine_layers = lax.dynamic_slice_in_dim(placed, rank * mine, mine)
    incoming = (
        lax.all_to_all(outgoing[0], "section", split_axis=0, concat_axis=0, tiled=True),
        lax.all_to_all(outgoing[1], "section", split_axis=0, concat_axis=0, tiled=True),
        lax.all_to_all(outgoing[2], "section", split_axis=0, concat_axis=0, tiled=True),
    )
    arranged = (incoming[0][anchor], incoming[1][anchor], incoming[2][anchor])
    state = (
        lax.all_to_all(arranged[0], "dp", split_axis=0, concat_axis=1, tiled=True),
        lax.all_to_all(arranged[1], "dp", split_axis=0, concat_axis=1, tiled=True),
        lax.all_to_all(arranged[2], "dp", split_axis=0, concat_axis=1, tiled=True),
    )
    result = adamw(state[0], state[1], state[2], grad, counts[mine_layers], full_columns)
    weight = result[0].reshape(-1, 1024)
    first = result[1].reshape(-1, 1024)
    second = result[2].reshape(-1, 1024)
    return (weight, first, second, weight.astype(jnp.bfloat16))


def solution(mesh):
    placed = (
        P("section", "dp"),
        P("section", "dp"),
        P("section", "dp"),
        P(("section", "dp"), None),
        P(),
        P(),
        P(),
    )
    return jax.shard_map(
        on_device,
        mesh=mesh,
        in_specs=placed,
        out_specs=(
            P(("section", "dp"), None),
            P(("section", "dp"), None),
            P(("section", "dp"), None),
            P(("section", "dp"), None),
        ),
        check_vma=False,
    )
```

profile of v0, /device:TPU:2, one launch (start us, length us, event | category | flops | bytes accessed | tf_op | source)
XLA Modules:
  0.0 186.9 jit_solution(13707104377042523516)
XLA Ops:
  3.1 0.9 gather_fusion.6
  4.0 2.0 %copy.21 = f32[16,1,16384]{2,1,0:T(1,128)} copy(f32[16,1,16384]{2,0,1:T(8,128)S(1)} %bitcast.40) | data formatting | bytes 2097152 | tf_op jit(solution)/shard_map/all_to_all | solution.py:56
  6.1 8.8 %all-to-all-start.4 = ((f32[16,1,16384]{2,1,0:T(1,128)}), f32[16,1,16384]{2,1,0:T(1,128)}, u32[]{:S(2)}, u32[]{:S(2)}) async-start(f32[16,1,16384]{2,1,0:T(1,128)} %copy.21), calls=%async_computation.4 | async-start | bytes 2097152 | tf_op jit(solution)/shard_map/all_to_all | solution.py:56
  14.9 0.9 gather_fusion.4
  15.8 2.0 %copy.19 = f32[16,1,16384]{2,1,0:T(1,128)} copy(f32[16,1,16384]{2,0,1:T(8,128)S(1)} %bitcast.41) | data formatting | bytes 2097152 | tf_op jit(solution)/shard_map/all_to_all | solution.py:55
  17.8 23.8 %all-to-all-done.4 = f32[16,1,16384]{2,1,0:T(1,128)} async-done(((f32[16,1,16384]{2,1,0:T(1,128)}), f32[16,1,16384]{2,1,0:T(1,128)}, u32[]{:S(2)}, u32[]{:S(2)}) %all-to-all-start.4) | async-done | bytes 1048608 | tf_op jit(solution)/shard_map/all_to_all | solution.py:56
  41.6 4.8 %all-to-all-start.2 = ((f32[16,1,16384]{2,1,0:T(1,128)}), f32[16,1,16384]{2,1,0:T(1,128)}, u32[]{:S(2)}, u32[]{:S(2)}) async-start(f32[16,1,16384]{2,1,0:T(1,128)} %copy.19), calls=%async_computation.2 | async-start | bytes 2097152 | tf_op jit(solution)/shard_map/all_to_all | solution.py:55
  46.4 0.9 gather_fusion.1
  47.3 2.0 %copy.17 = f32[16,1,16384]{2,1,0:T(1,128)} copy(f32[16,1,16384]{2,0,1:T(8,128)S(1)} %bitcast.37) | data formatting | bytes 2097152 | tf_op jit(solution)/shard_map/all_to_all | solution.py:54
  49.4 23.7 %all-to-all-done.2 = f32[16,1,16384]{2,1,0:T(1,128)} async-done(((f32[16,1,16384]{2,1,0:T(1,128)}), f32[16,1,16384]{2,1,0:T(1,128)}, u32[]{:S(2)}, u32[]{:S(2)}) %all-to-all-start.2) | async-done | bytes 1048608 | tf_op jit(solution)/shard_map/all_to_all | solution.py:55
  73.1 4.9 %all-to-all-start = ((f32[16,1,16384]{2,1,0:T(1,128)}), f32[16,1,16384]{2,1,0:T(1,128)}, u32[]{:S(2)}, u32[]{:S(2)}) async-start(f32[16,1,16384]{2,1,0:T(1,128)} %copy.17), calls=%async_computation | async-start | bytes 2097152 | tf_op jit(solution)/shard_map/all_to_all | solution.py:54
  78.8 1.8 copy.29
  80.6 0.9 gather_fusion.7
  81.5 2.0 %copy.22 = f32[16,1,16384]{2,1,0:T(1,128)} copy(f32[16,1,16384]{2,0,1:T(8,128)S(1)} %bitcast.38) | data formatting | bytes 2097152 | tf_op jit(solution)/shard_map/all_to_all | solution.py:62
  83.6 21.1 %all-to-all-done = f32[16,1,16384]{2,1,0:T(1,128)} async-done(((f32[16,1,16384]{2,1,0:T(1,128)}), f32[16,1,16384]{2,1,0:T(1,128)}, u32[]{:S(2)}, u32[]{:S(2)}) %all-to-all-start) | async-done | bytes 1048608 | tf_op jit(solution)/shard_map/all_to_all | solution.py:54
  104.7 7.5 %all-to-all-start.5 = ((f32[16,1,16384]{2,1,0:T(1,128)}), f32[16,1,16384]{2,1,0:T(1,128)}, u32[]{:S(2)}, u32[]{:S(2)}) async-start(f32[16,1,16384]{2,1,0:T(1,128)} %copy.22), calls=%async_computation.5 | async-start | bytes 2097152 | tf_op jit(solution)/shard_map/all_to_all | solution.py:62
  112.1 1.8 copy.30
  114.0 0.9 gather_fusion.5
  114.9 2.0 %copy.20 = f32[16,1,16384]{2,1,0:T(1,128)} copy(f32[16,1,16384]{2,0,1:T(8,128)S(1)} %bitcast.39) | data formatting | bytes 2097152 | tf_op jit(solution)/shard_map/all_to_all | solution.py:61
  116.9 12.2 %all-to-all-done.5 = f32[16,1,16384]{2,1,0:T(1,128)} async-done(((f32[16,1,16384]{2,1,0:T(1,128)}), f32[16,1,16384]{2,1,0:T(1,128)}, u32[]{:S(2)}, u32[]{:S(2)}) %all-to-all-start.5) | async-done | bytes 1048608 | tf_op jit(solution)/shard_map/all_to_all | solution.py:62
  129.2 7.5 %all-to-all-start.3 = ((f32[16,1,16384]{2,1,0:T(1,128)}), f32[16,1,16384]{2,1,0:T(1,128)}, u32[]{:S(2)}, u32[]{:S(2)}) async-start(f32[16,1,16384]{2,1,0:T(1,128)} %copy.20), calls=%async_computation.3 | async-start | bytes 2097152 | tf_op jit(solution)/shard_map/all_to_all | solution.py:61
  136.6 1.8 copy.31
  138.5 0.9 gather_fusion.3
  139.4 2.0 %copy.18 = f32[16,1,16384]{2,1,0:T(1,128)} copy(f32[16,1,16384]{2,0,1:T(8,128)S(1)} %bitcast.36) | data formatting | bytes 2097152 | tf_op jit(solution)/shard_map/all_to_all | solution.py:60
  141.4 11.8 %all-to-all-done.3 = f32[16,1,16384]{2,1,0:T(1,128)} async-done(((f32[16,1,16384]{2,1,0:T(1,128)}), f32[16,1,16384]{2,1,0:T(1,128)}, u32[]{:S(2)}, u32[]{:S(2)}) %all-to-all-start.3) | async-done | bytes 1048608 | tf_op jit(solution)/shard_map/all_to_all | solution.py:61
  153.3 6.3 %all-to-all-start.1 = ((f32[16,1,16384]{2,1,0:T(1,128)}), f32[16,1,16384]{2,1,0:T(1,128)}, u32[]{:S(2)}, u32[]{:S(2)}) async-start(f32[16,1,16384]{2,1,0:T(1,128)} %copy.18), calls=%async_computation.1 | async-start | bytes 2097152 | tf_op jit(solution)/shard_map/all_to_all | solution.py:60
  163.4 4.4 %multiply_reduce_fusion = f32[16,16384]{1,0:T(8,128)S(1)} fusion(f32[16,1,16384]{2,1,0:T(1,128)} %all-to-all-done.5), kind=kLoop, calls=%fused_computation.14 | loop fusion | flops 262144 | bytes 2097152 | tf_op jit(solution)/shard_map/mul | solution.py:16
  168.0 5.2 %multiply_reduce_fusion.1 = f32[16,16384]{1,0:T(8,128)} fusion(f32[16,1,16384]{2,1,0:T(1,128)} %all-to-all-done.3), kind=kLoop, calls=%fused_computation.16 | loop fusion | flops 262144 | bytes 2097152 | tf_op jit(solution)/shard_map/mul | solution.py:15
  173.2 1.4 mul.77
  175.0 4.7 %reduce = f32[16,16384]{1,0:T(8,128)} reduce(f32[16,1,16384]{2,1,0:T(1,128)} %all-to-all-done.1, f32[]{:T(128)} %constant.83), dimensions={1}, to_apply=%all_to_all.60.reduce_sub_computation | reduce | bytes 2097156 | tf_op jit(solution)/shard_map/all_to_all | solution.py:60
  179.7 2.4 %all_to_all.61 = f32[256,1024]{1,0:T(8,128)} reshape(f32[16,16384]{1,0:T(8,128)} %reduce) | data formatting | bytes 2097152 | tf_op jit(solution)/shard_map/all_to_all | solution.py:60
  182.1 4.8 %fusion.5 = (bf16[256,1024]{1,0:T(8,128)(2,1)}, f32[256,1024]{1,0:T(8,128)}, f32[256,1024]{1,0:T(8,128)}, f32[256,1024]{1,0:T(8,128)}) fusion(f32[256,1024]{1,0:T(8,128)} %all_to_all.61, f32[256,1024]{1,0:T(8,128)S(1)} %mul.81, f32[256,1024]{1,0:T(8,128)} %param.10, f32[256,1024]{1,0:T(8,128)S(1)} %mul.77, s32[]{:T(128)} %bitcast.1), kind=kLoop, calls=%fused_computation.45 | loop fusion | flops 4718592 | bytes 7864324 | tf_op jit(solution)/shard_map/convert_element_type | solution.py:68
  (29 shorter events, 5.7 us)
Async XLA Ops:
  0.6 2.5 %copy-start = (f32[16,16384]{1,0:T(8,128)S(1)}, f32[16,16384]{1,0:T(8,128)}, u32[]{:S(2)}) copy-start(f32[16,16384]{1,0:T(8,128)} %param.9) | copy-start | bytes 3145732
  0.7 0.8 copy-start.4
  1.5 0.7 copy-start.3
  6.1 8.8 %copy-start.1 = (f32[16,16384]{1,0:T(8,128)S(1)}, f32[16,16384]{1,0:T(8,128)}, u32[]{:S(2)}) copy-start(f32[16,16384]{1,0:T(8,128)} %param.8) | copy-start | bytes 3145732
  6.1 35.5 %all-to-all-start.4 = ((f32[16,1,16384]{2,1,0:T(1,128)}), f32[16,1,16384]{2,1,0:T(1,128)}, u32[]{:S(2)}, u32[]{:S(2)}) async-start(f32[16,1,16384]{2,1,0:T(1,128)} %copy.21), calls=%async_computation.4 | async-start | bytes 2097152 | tf_op jit(solution)/shard_map/all_to_all | solution.py:56
  17.8 28.6 %copy-start.2 = (f32[16,16384]{1,0:T(8,128)S(1)}, f32[16,16384]{1,0:T(8,128)}, u32[]{:S(2)}) copy-start(f32[16,16384]{1,0:T(8,128)} %param.7) | copy-start | bytes 3145732
  41.6 31.5 %all-to-all-start.2 = ((f32[16,1,16384]{2,1,0:T(1,128)}), f32[16,1,16384]{2,1,0:T(1,128)}, u32[]{:S(2)}, u32[]{:S(2)}) async-start(f32[16,1,16384]{2,1,0:T(1,128)} %copy.19), calls=%async_computation.2 | async-start | bytes 2097152 | tf_op jit(solution)/shard_map/all_to_all | solution.py:55
  73.1 31.6 %all-to-all-start = ((f32[16,1,16384]{2,1,0:T(1,128)}), f32[16,1,16384]{2,1,0:T(1,128)}, u32[]{:S(2)}, u32[]{:S(2)}) async-start(f32[16,1,16384]{2,1,0:T(1,128)} %copy.17), calls=%async_computation | async-start | bytes 2097152 | tf_op jit(solution)/shard_map/all_to_all | solution.py:54
  104.7 24.5 %all-to-all-start.5 = ((f32[16,1,16384]{2,1,0:T(1,128)}), f32[16,1,16384]{2,1,0:T(1,128)}, u32[]{:S(2)}, u32[]{:S(2)}) async-start(f32[16,1,16384]{2,1,0:T(1,128)} %copy.22), calls=%async_computation.5 | async-start | bytes 2097152 | tf_op jit(solution)/shard_map/all_to_all | solution.py:62
  129.2 24.1 %all-to-all-start.3 = ((f32[16,1,16384]{2,1,0:T(1,128)}), f32[16,1,16384]{2,1,0:T(1,128)}, u32[]{:S(2)}, u32[]{:S(2)}) async-start(f32[16,1,16384]{2,1,0:T(1,128)} %copy.20), calls=%async_computation.3 | async-start | bytes 2097152 | tf_op jit(solution)/shard_map/all_to_all | solution.py:61
  153.3 21.7 %all-to-all-start.1 = ((f32[16,1,16384]{2,1,0:T(1,128)}), f32[16,1,16384]{2,1,0:T(1,128)}, u32[]{:S(2)}, u32[]{:S(2)}) async-start(f32[16,1,16384]{2,1,0:T(1,128)} %copy.18), calls=%async_computation.1 | async-start | bytes 2097152 | tf_op jit(solution)/shard_map/all_to_all | solution.py:60
  162.1 0.7 copy-start.5
where the time goes:
time: 188 us; the launch traced here: 187 us
  waiting for transfers between devices  93 us (49%)
  starting transfers between devices  39.7 us (21%)
  local copies, waits for them, and re-layouts  31.8 us (17%)
  other arithmetic  19.6 us (10%)
  between operations  2.78 us (1%)
    all_to_all x1, waiting for transfers between devices, on_device(): lax.all_to_all(outgoing[2], 'section', split_axis=0, concat_axis=0, tiled...  23.8 us
    all_to_all x1, waiting for transfers between devices, on_device(): lax.all_to_all(outgoing[1], 'section', split_axis=0, concat_axis=0, tiled...  23.7 us
    all_to_all x1, waiting for transfers between devices, on_device(): lax.all_to_all(outgoing[0], 'section', split_axis=0, concat_axis=0, tiled...  21.1 us
    all_to_all x1, waiting for transfers between devices, on_device(): lax.all_to_all(arranged[2], 'dp', split_axis=0, concat_axis=1, tiled=True)  12.2 us
    all_to_all x1, waiting for transfers between devices, on_device(): lax.all_to_all(arranged[1], 'dp', split_axis=0, concat_axis=1, tiled=True)  11.8 us
    all_to_all x1, starting transfers between devices, on_device(): lax.all_to_all(outgoing[2], 'section', split_axis=0, concat_axis=0, tiled...  8.75 us
    unnamed x15, local copies, waits for them, and re-layouts  7.63 us
    all_to_all x1, starting transfers between devices, on_device(): lax.all_to_all(arranged[2], 'dp', split_axis=0, concat_axis=1, tiled=True)  7.48 us
  transfers between devices with their start and end apart: 6, of which 6 were waited for; matrix products, arithmetic and copies ran while one was open for 18% of the time, Pallas kernels for 0%

commit v1 on v0

v1 whole, which is shorter than its diff:
```python
import functools

import jax
import jax.numpy as jnp
from jax import lax
from jax.experimental import pallas as pl
from jax.experimental.pallas import tpu as pltpu
from jax.sharding import PartitionSpec as P

STEP = 1000
LANES = 128
SUBLANES = 8
AXES = ("section", "dp")
ROUNDS = ((0, 0), (2, 0), (1, 0), (3, 0), (0, 1), (2, 1), (1, 1), (3, 1))
FIRST_SWAP = 6


def target(old_section, block, shift, flip):
    z, core = old_section >> 1, old_section & 1
    y, x = block >> 2, block & 3
    turn = 2 * ((y + shift) & 3) + ((x & 1) ^ flip)
    odd = (z & 1) ^ core
    move = (turn + odd * (4 - 2 * turn)) * (1 - 2 * core)
    return 2 * ((z + move) & 7) + (core ^ (x >> 1))


def origin(old_section, new_section, shift, flip):
    z, core = old_section >> 1, old_section & 1
    move = ((new_section >> 1) - z) * (1 - 2 * core)
    odd = (z & 1) ^ core
    turn = (move + odd * (4 - 2 * move)) & 7
    y = ((turn >> 1) - shift) & 3
    x = 2 * (core ^ (new_section & 1)) + ((turn & 1) ^ flip)
    return 4 * y + x


def round_pairs(shift, flip):
    pairs = []
    for section in range(16):
        for rank in range(16):
            there = target(section, rank, shift, flip)
            pairs.append((section * 16 + rank, there * 16 + section))
    return pairs


SWAP = [(s * 16 + r, (s ^ 1) * 16 + r) for s in range(16) for r in range(16)]


def pack_kernel(slots, old_ref, new_ref, *refs):
    states, messages = refs[:3], refs[3 : 3 + len(ROUNDS)]
    row_of, tiles = refs[3 + len(ROUNDS)], refs[4 + len(ROUNDS) :]
    section, rank = lax.axis_index("section"), lax.axis_index("dp")
    columns = states[0].shape[1] // LANES
    for slot in range(slots):
        row_of[old_ref[section * slots + slot]] = slot
    for state, tile in zip(states, tiles):
        for half in range(slots // SUBLANES):
            for column in range(columns):
                tile[pl.ds((half * columns + column) * SUBLANES, SUBLANES), :] = state[
                    pl.ds(half * SUBLANES, SUBLANES), pl.ds(column * LANES, LANES)
                ]
    for message, (shift, flip) in zip(messages, ROUNDS):
        there = target(section, rank, shift, flip)
        for part in range(2):
            row = row_of[new_ref[(there ^ part) * slots + section]]
            start = (row >> 3) * (columns * SUBLANES) + (row & 7)
            for index, tile in enumerate(tiles):
                for half in range(2):
                    for column in range(8):
                        message[
                            pl.ds((part * 3 + index) * 16 + half * SUBLANES, SUBLANES),
                            pl.ds(column * LANES, LANES),
                        ] = tile[
                            pl.ds(start + (64 * half + column) * SUBLANES, SUBLANES, stride=64), :
                        ]


def adamw(weight, first, second, grad, live):
    first = 0.9 * first + 0.1 * grad
    second = 0.95 * second + 0.05 * grad * grad
    step_size = first / (1.0 - 0.9**STEP) / (jnp.sqrt(second / (1.0 - 0.95**STEP)) + 1e-08)
    weight = weight - 0.01 * (step_size + 0.1 * weight)
    zero = jnp.float32(0.0)
    return (
        jnp.where(live, weight, zero),
        jnp.where(live, first, zero),
        jnp.where(live, second, zero),
    )


def update_kernel(slots, counts_ref, new_ref, grads, *refs):
    kept, swapped = refs[: len(ROUNDS)], refs[len(ROUNDS) : len(ROUNDS) + 2]
    outs = refs[len(ROUNDS) + 2 :]
    section, rank = lax.axis_index("section"), lax.axis_index("dp")
    limit = counts_ref[new_ref[section * slots + rank]]
    width = grads.shape[1]
    place = width * lax.broadcasted_iota(jnp.int32, (16, width), 0) + lax.broadcasted_iota(
        jnp.int32, (16, width), 1
    )
    for number, (shift, flip) in enumerate(ROUNDS):
        block = origin(rank, section, shift, flip)
        if number < FIRST_SWAP:
            other = swapped[0].at[pl.ds(48 * number, 48)]
        else:
            other = swapped[1].at[pl.ds(48 * (number - FIRST_SWAP), 48)]
        for held, spot in ((kept[number], block), (other, block ^ 2)):
            rows = pl.ds(pl.multiple_of(spot * 16, 16), 16)
            live = place < limit - spot * (16 * width)
            weight, first, second = adamw(
                held[pl.ds(0, 16), :], held[pl.ds(16, 16), :], held[pl.ds(32, 16), :], grads[rows, :], live
            )
            outs[0][rows, :] = weight
            outs[1][rows, :] = first
            outs[2][rows, :] = second
            outs[3][rows, :] = weight.astype(jnp.bfloat16)


def on_device(master, momentum, variance, grads, counts, old_layers, new_layers):
    slots, columns = master.shape
    vmem = pl.BlockSpec(memory_space=pltpu.VMEM)
    smem = pl.BlockSpec(memory_space=pltpu.SMEM)
    params = pltpu.CompilerParams(vmem_limit_bytes=40 * 2**20)
    messages = pl.pallas_call(
        functools.partial(pack_kernel, slots),
        out_shape=[jax.ShapeDtypeStruct((96, 1024), jnp.float32)] * len(ROUNDS),
        in_specs=[smem, smem, vmem, vmem, vmem],
        out_specs=[vmem] * len(ROUNDS),
        scratch_shapes=[pltpu.SMEM((old_layers.shape[0],), jnp.int32)]
        + [pltpu.VMEM((slots * columns // LANES, LANES), jnp.float32)] * 3,
        compiler_params=params,
    )(old_layers, new_layers, master, momentum, variance)
    arrived = [
        lax.ppermute(message, AXES, round_pairs(*turn)) for message, turn in zip(messages, ROUNDS)
    ]
    swapped = [
        lax.ppermute(jnp.concatenate([got[48:] for got in group]), AXES, SWAP)
        for group in (arrived[:FIRST_SWAP], arrived[FIRST_SWAP:])
    ]
    return tuple(
        pl.pallas_call(
            functools.partial(update_kernel, slots),
            out_shape=[jax.ShapeDtypeStruct(grads.shape, jnp.float32)] * 3
            + [jax.ShapeDtypeStruct(grads.shape, jnp.bfloat16)],
            in_specs=[smem, smem] + [vmem] * (len(ROUNDS) + 3),
            out_specs=[vmem] * 4,
            compiler_params=params,
        )(counts, new_layers, grads, *arrived, *swapped)
    )


def solution(mesh):
    placed = (
        P("section", "dp"),
        P("section", "dp"),
        P("section", "dp"),
        P(("section", "dp"), None),
        P(),
        P(),
        P(),
    )
    return jax.shard_map(
        on_device,
        mesh=mesh,
        in_specs=placed,
        out_specs=(
            P(("section", "dp"), None),
            P(("section", "dp"), None),
            P(("section", "dp"), None),
            P(("section", "dp"), None),
        ),
        check_vma=False,
    )
```

time: 188 us -> 110 us (0.59)
  the two profiles are of different devices: /device:TPU:2 before, /device:TPU:23 now
where the time goes in v1:
time: 110 us; the launch traced here: 109 us
  waiting for transfers between devices  55.5 us (50%)
  starting transfers between devices  41.6 us (38%)
  Pallas kernels  6.08 us (6%)
  local copies, waits for them, and re-layouts  5.16 us (5%)
    ppermute x8, waiting for transfers between devices, on_device(): lax.ppermute(message, AXES, round_pairs(*turn))  53.8 us
    ppermute x8, starting transfers between devices, on_device(): lax.ppermute(message, AXES, round_pairs(*turn))  41.4 us
    unnamed x21, local copies, waits for them, and re-layouts  5.12 us
    pallas_call x1, Pallas kernels, on_device(): pl.pallas_call(functools.partial(update_kernel, slots), out_shape=[jax.Sh...  3.46 us
    pallas_call x1, Pallas kernels, on_device(): pl.pallas_call(functools.partial(pack_kernel, slots), out_shape=[jax.Shap...  2.62 us
  transfers between devices with their start and end apart: 10, of which 6 were waited for; matrix products, arithmetic and copies ran while one was open for 0% of the time, Pallas kernels for 0%

profile of v1, /device:TPU:23, one launch (start us, length us, event | category | flops | bytes accessed | tf_op | source)
XLA Modules:
  0.0 109.2 jit_solution(455179650307629267)
XLA Ops:
  0.6 0.0 copy-start
  0.6 1.2 %copy-done = f32[16,16384]{1,0:T(8,128)S(1)} copy-done((f32[16,16384]{1,0:T(8,128)S(1)}, f32[16,16384]{1,0:T(8,128)}, u32[]{:S(2)}) %copy-start) | copy-done | bytes 1048600
  1.9 1.2 %copy-done.1 = f32[16,16384]{1,0:T(8,128)S(1)} copy-done((f32[16,16384]{1,0:T(8,128)S(1)}, f32[16,16384]{1,0:T(8,128)}, u32[]{:S(2)}) %copy-start.1) | copy-done | bytes 1048600
  3.1 1.2 %copy-done.2 = f32[16,16384]{1,0:T(8,128)S(1)} copy-done((f32[16,16384]{1,0:T(8,128)S(1)}, f32[16,16384]{1,0:T(8,128)}, u32[]{:S(2)}) %copy-start.2) | copy-done | bytes 1048600
  4.3 0.7 copy-done.4
  5.0 0.7 copy-done.6
  5.7 2.6 %shard_map.102 = (f32[96,1024]{1,0:T(8,128)S(1)}, f32[96,1024]{1,0:T(8,128)S(1)}, f32[96,1024]{1,0:T(8,128)S(1)}, f32[96,1024]{1,0:T(8,128)S(1)}, f32[96,1024]{1...) custom-call(s32[256]{0:T(256)S(1)} %copy-done.6, s32[256]{0:T(256)S(1)} %copy-done.4, ...), custom_call_target="tpu_custom_call" | custom-call | tf_op jit(solution)/shard_map/pallas_call | solution.py:123
  8.3 4.7 %collective-permute-start = (f32[96,1024]{1,0:T(8,128)S(1)}, f32[96,1024]{1,0:T(8,128)S(1)}, u32[]{:S(2)}, u32[]{:S(2)}) collective-permute-start(f32[96,1024]{1,0:T(8,128)S(1)} %get-tuple-element.12), channel_id=1, source_target_pairs={{0,0},{1,32},{2,16},{3,48},{4,64},{5,96},{6,80},{7,112},{8,128},{9... | collective-permute-start | bytes 1179656 | tf_op jit(solution)/shard_map/ppermute | solution.py:133
  13.0 8.6 %collective-permute-start.1 = (f32[96,1024]{1,0:T(8,128)S(1)}, f32[96,1024]{1,0:T(8,128)S(1)}, u32[]{:S(2)}, u32[]{:S(2)}) collective-permute-start(f32[96,1024]{1,0:T(8,128)S(1)} %get-tuple-element.13), channel_id=1, source_target_pairs={{0,128},{1,160},{2,144},{3,176},{4,192},{5,224},{6,208},{7,240},{8... | collective-permute-start | bytes 1179656 | tf_op jit(solution)/shard_map/ppermute | solution.py:133
  21.6 3.9 %collective-permute-start.2 = (f32[96,1024]{1,0:T(8,128)S(1)}, f32[96,1024]{1,0:T(8,128)S(1)}, u32[]{:S(2)}, u32[]{:S(2)}) collective-permute-start(f32[96,1024]{1,0:T(8,128)S(1)} %get-tuple-element.14), channel_id=1, source_target_pairs={{0,64},{1,96},{2,80},{3,112},{4,128},{5,160},{6,144},{7,176},{8,19... | collective-permute-start | bytes 1179656 | tf_op jit(solution)/shard_map/ppermute | solution.py:133
  25.6 7.3 %collective-permute-start.3 = (f32[96,1024]{1,0:T(8,128)S(1)}, f32[96,1024]{1,0:T(8,128)S(1)}, u32[]{:S(2)}, u32[]{:S(2)}) collective-permute-start(f32[96,1024]{1,0:T(8,128)S(1)} %get-tuple-element.15), channel_id=1, source_target_pairs={{0,192},{1,224},{2,208},{3,240},{4,0},{5,32},{6,16},{7,48},{8,64},... | collective-permute-start | bytes 1179656 | tf_op jit(solution)/shard_map/ppermute | solution.py:133
  32.8 1.9 %collective-permute-start.4 = (f32[96,1024]{1,0:T(8,128)S(1)}, f32[96,1024]{1,0:T(8,128)S(1)}, u32[]{:S(2)}, u32[]{:S(2)}) collective-permute-start(f32[96,1024]{1,0:T(8,128)S(1)} %get-tuple-element.16), channel_id=1, source_target_pairs={{0,32},{1,0},{2,48},{3,16},{4,96},{5,64},{6,112},{7,80},{8,160},{9... | collective-permute-start | bytes 1179656 | tf_op jit(solution)/shard_map/ppermute | solution.py:133
  34.8 0.0 collective-permute-done.refs_0_
  34.8 6.5 %collective-permute-start.5 = (f32[96,1024]{1,0:T(8,128)S(1)}, f32[96,1024]{1,0:T(8,128)S(1)}, u32[]{:S(2)}, u32[]{:S(2)}) collective-permute-start(f32[96,1024]{1,0:T(8,128)S(1)} %get-tuple-element.17), channel_id=1, source_target_pairs={{0,160},{1,128},{2,176},{3,144},{4,224},{5,192},{6,240},{7,208},{8... | collective-permute-start | bytes 1179656 | tf_op jit(solution)/shard_map/ppermute | solution.py:133
  41.3 0.0 collective-permute-done.1.refs_1_
  41.3 19.1 %collective-permute-done.2.refs_2_ = f32[96,1024]{1,0:T(8,128)S(1)} collective-permute-done((f32[96,1024]{1,0:T(8,128)S(1)}, f32[96,1024]{1,0:T(8,128)S(1)}, u32[]{:S(2)}, u32[]{:S(2)}) %collective-permute-start.2) | collective-permute-done | bytes 393248 | tf_op jit(solution)/shard_map/ppermute | solution.py:133
  60.4 7.6 %collective-permute-done.3.refs_3_ = f32[96,1024]{1,0:T(8,128)S(1)} collective-permute-done((f32[96,1024]{1,0:T(8,128)S(1)}, f32[96,1024]{1,0:T(8,128)S(1)}, u32[]{:S(2)}, u32[]{:S(2)}) %collective-permute-start.3) | collective-permute-done | bytes 393248 | tf_op jit(solution)/shard_map/ppermute | solution.py:133
  68.0 0.0 copy-start.3
  68.0 0.0 copy-start.5
  68.0 0.0 copy-start.7
  68.0 0.0 collective-permute-done.4.refs_4_
  68.1 6.9 %collective-permute-done.5.refs_5_ = f32[96,1024]{1,0:T(8,128)S(1)} collective-permute-done((f32[96,1024]{1,0:T(8,128)S(1)}, f32[96,1024]{1,0:T(8,128)S(1)}, u32[]{:S(2)}, u32[]{:S(2)}) %collective-permute-start.5) | collective-permute-done | bytes 393248 | tf_op jit(solution)/shard_map/ppermute | solution.py:133
  74.9 0.1 collective-permute-start.8
  75.0 1.9 %collective-permute-start.6 = (f32[96,1024]{1,0:T(8,128)S(1)}, f32[96,1024]{1,0:T(8,128)S(1)}, u32[]{:S(2)}, u32[]{:S(2)}) collective-permute-start(f32[96,1024]{1,0:T(8,128)S(1)} %get-tuple-element.18), channel_id=1, source_target_pairs={{0,96},{1,64},{2,112},{3,80},{4,160},{5,128},{6,176},{7,144},{8,22... | collective-permute-start | bytes 1179656 | tf_op jit(solution)/shard_map/ppermute | solution.py:133
  77.0 6.5 %collective-permute-start.7 = (f32[96,1024]{1,0:T(8,128)S(1)}, f32[96,1024]{1,0:T(8,128)S(1)}, u32[]{:S(2)}, u32[]{:S(2)}) collective-permute-start(f32[96,1024]{1,0:T(8,128)S(1)} %get-tuple-element.19), channel_id=1, source_target_pairs={{0,224},{1,192},{2,240},{3,208},{4,32},{5,0},{6,48},{7,16},{8,96},... | collective-permute-start | bytes 1179656 | tf_op jit(solution)/shard_map/ppermute | solution.py:133
  83.5 10.1 %collective-permute-done.6.refs_6_ = f32[96,1024]{1,0:T(8,128)S(1)} collective-permute-done((f32[96,1024]{1,0:T(8,128)S(1)}, f32[96,1024]{1,0:T(8,128)S(1)}, u32[]{:S(2)}, u32[]{:S(2)}) %collective-permute-start.6) | collective-permute-done | bytes 393248 | tf_op jit(solution)/shard_map/ppermute | solution.py:133
  93.6 10.3 %collective-permute-done.7.refs_7_ = f32[96,1024]{1,0:T(8,128)S(1)} collective-permute-done((f32[96,1024]{1,0:T(8,128)S(1)}, f32[96,1024]{1,0:T(8,128)S(1)}, u32[]{:S(2)}, u32[]{:S(2)}) %collective-permute-start.7) | collective-permute-done | bytes 393248 | tf_op jit(solution)/shard_map/ppermute | solution.py:133
  103.9 0.1 collective-permute-start.9
  104.0 1.7 %collective-permute-done.9.refs_9_ = f32[96,1024]{1,0:T(8,128)S(1)} collective-permute-done((f32[96,1024]{1,0:T(8,128)S(1)}, f32[96,1024]{1,0:T(8,128)S(1)}, u32[]{:S(2)}, u32[]{:S(2)}) %collective-permute-start.9) | collective-permute-done | bytes 393248 | tf_op jit(solution)/shard_map/ppermute | solution.py:136
  105.7 0.0 collective-permute-done.8.refs_8_
  105.7 0.0 copy-done.7
  105.8 3.5 %shard_map.103 = (f32[256,1024]{1,0:T(8,128)}, f32[256,1024]{1,0:T(8,128)}, f32[256,1024]{1,0:T(8,128)}, bf16[256,1024]{1,0:T(8,128)(2,1)}) custom-call(s32[256]{0:T(256)S(1)} %copy-done.7, s32[256]{0:T(256)S(1)} %copy-done.5, f32[256,1024]{1,0:T(8,128)S(1)} %copy-done.3, f32[96,1024]{1,0:T(8,128)S(1)} %collective-permute-done.refs_0_, ...), custom_call_target="tpu_custom_call" | custom-call | tf_op jit(solution)/shard_map/pallas_call | solution.py:140
  (15 shorter events, 0.2 us)
Async XLA Ops:
  0.6 1.2 %copy-start = (f32[16,16384]{1,0:T(8,128)S(1)}, f32[16,16384]{1,0:T(8,128)}, u32[]{:S(2)}) copy-start(f32[16,16384]{1,0:T(8,128)} %refs_0_.1) | copy-start | bytes 3145732
  1.9 1.2 %copy-start.1 = (f32[16,16384]{1,0:T(8,128)S(1)}, f32[16,16384]{1,0:T(8,128)}, u32[]{:S(2)}) copy-start(f32[16,16384]{1,0:T(8,128)} %refs_1_.1) | copy-start | bytes 3145732
  3.1 1.2 %copy-start.2 = (f32[16,16384]{1,0:T(8,128)S(1)}, f32[16,16384]{1,0:T(8,128)}, u32[]{:S(2)}) copy-start(f32[16,16384]{1,0:T(8,128)} %refs_2_.1) | copy-start | bytes 3145732
  4.3 0.7 copy-start.4
  5.0 0.7 copy-start.6
  8.3 26.5 %collective-permute-start = (f32[96,1024]{1,0:T(8,128)S(1)}, f32[96,1024]{1,0:T(8,128)S(1)}, u32[]{:S(2)}, u32[]{:S(2)}) collective-permute-start(f32[96,1024]{1,0:T(8,128)S(1)} %get-tuple-element.12), channel_id=1, source_target_pairs={{0,0},{1,32},{2,16},{3,48},{4,64},{5,96},{6,80},{7,112},{8,128},{9... | collective-permute-start | bytes 1179656 | tf_op jit(solution)/shard_map/ppermute | solution.py:133
  13.0 28.3 %collective-permute-start.1 = (f32[96,1024]{1,0:T(8,128)S(1)}, f32[96,1024]{1,0:T(8,128)S(1)}, u32[]{:S(2)}, u32[]{:S(2)}) collective-permute-start(f32[96,1024]{1,0:T(8,128)S(1)} %get-tuple-element.13), channel_id=1, source_target_pairs={{0,128},{1,160},{2,144},{3,176},{4,192},{5,224},{6,208},{7,240},{8... | collective-permute-start | bytes 1179656 | tf_op jit(solution)/shard_map/ppermute | solution.py:133
  21.6 38.8 %collective-permute-start.2 = (f32[96,1024]{1,0:T(8,128)S(1)}, f32[96,1024]{1,0:T(8,128)S(1)}, u32[]{:S(2)}, u32[]{:S(2)}) collective-permute-start(f32[96,1024]{1,0:T(8,128)S(1)} %get-tuple-element.14), channel_id=1, source_target_pairs={{0,64},{1,96},{2,80},{3,112},{4,128},{5,160},{6,144},{7,176},{8,19... | collective-permute-start | bytes 1179656 | tf_op jit(solution)/shard_map/ppermute | solution.py:133
  25.6 42.4 %collective-permute-start.3 = (f32[96,1024]{1,0:T(8,128)S(1)}, f32[96,1024]{1,0:T(8,128)S(1)}, u32[]{:S(2)}, u32[]{:S(2)}) collective-permute-start(f32[96,1024]{1,0:T(8,128)S(1)} %get-tuple-element.15), channel_id=1, source_target_pairs={{0,192},{1,224},{2,208},{3,240},{4,0},{5,32},{6,16},{7,48},{8,64},... | collective-permute-start | bytes 1179656 | tf_op jit(solution)/shard_map/ppermute | solution.py:133
  32.8 35.2 %collective-permute-start.4 = (f32[96,1024]{1,0:T(8,128)S(1)}, f32[96,1024]{1,0:T(8,128)S(1)}, u32[]{:S(2)}, u32[]{:S(2)}) collective-permute-start(f32[96,1024]{1,0:T(8,128)S(1)} %get-tuple-element.16), channel_id=1, source_target_pairs={{0,32},{1,0},{2,48},{3,16},{4,96},{5,64},{6,112},{7,80},{8,160},{9... | collective-permute-start | bytes 1179656 | tf_op jit(solution)/shard_map/ppermute | solution.py:133
  34.8 40.2 %collective-permute-start.5 = (f32[96,1024]{1,0:T(8,128)S(1)}, f32[96,1024]{1,0:T(8,128)S(1)}, u32[]{:S(2)}, u32[]{:S(2)}) collective-permute-start(f32[96,1024]{1,0:T(8,128)S(1)} %get-tuple-element.17), channel_id=1, source_target_pairs={{0,160},{1,128},{2,176},{3,144},{4,224},{5,192},{6,240},{7,208},{8... | collective-permute-start | bytes 1179656 | tf_op jit(solution)/shard_map/ppermute | solution.py:133
  68.0 37.7 %copy-start.3 = (f32[256,1024]{1,0:T(8,128)S(1)}, f32[256,1024]{1,0:T(8,128)}, u32[]{:S(2)}) copy-start(f32[256,1024]{1,0:T(8,128)} %grads.1) | copy-start | bytes 3145732
  68.0 37.7 %copy-start.5 = (s32[256]{0:T(256)S(1)}, s32[256]{0:T(256)}, u32[]{:S(2)}) copy-start(s32[256]{0:T(256)} %new_ref.3) | copy-start | bytes 3076
  68.0 37.7 %copy-start.7 = (s32[256]{0:T(256)S(1)}, s32[256]{0:T(256)}, u32[]{:S(2)}) copy-start(s32[256]{0:T(256)} %counts_ref.1) | copy-start | bytes 3076
  74.9 30.8 %collective-permute-start.8 = (f32[288,1024]{1,0:T(8,128)S(1)}, f32[288,1024]{1,0:T(8,128)S(1)}, u32[]{:S(2)}, u32[]{:S(2)}) collective-permute-start(f32[288,1024]{1,0:T(8,128)S(1)} %slice_dynamic-update-slice_fusion), channel_id=1, source_target_pairs={{0,16},{1,17},{2,18},{3,19},{4,20},{5,21},{6,22},{7,23},{8,24},{9,... | collective-permute-start | bytes 3538952 | tf_op jit(solution)/shard_map/ppermute | solution.py:136
  75.0 18.5 %collective-permute-start.6 = (f32[96,1024]{1,0:T(8,128)S(1)}, f32[96,1024]{1,0:T(8,128)S(1)}, u32[]{:S(2)}, u32[]{:S(2)}) collective-permute-start(f32[96,1024]{1,0:T(8,128)S(1)} %get-tuple-element.18), channel_id=1, source_target_pairs={{0,96},{1,64},{2,112},{3,80},{4,160},{5,128},{6,176},{7,144},{8,22... | collective-permute-start | bytes 1179656 | tf_op jit(solution)/shard_map/ppermute | solution.py:133
  77.0 26.9 %collective-permute-start.7 = (f32[96,1024]{1,0:T(8,128)S(1)}, f32[96,1024]{1,0:T(8,128)S(1)}, u32[]{:S(2)}, u32[]{:S(2)}) collective-permute-start(f32[96,1024]{1,0:T(8,128)S(1)} %get-tuple-element.19), channel_id=1, source_target_pairs={{0,224},{1,192},{2,240},{3,208},{4,32},{5,0},{6,48},{7,16},{8,96},... | collective-permute-start | bytes 1179656 | tf_op jit(solution)/shard_map/ppermute | solution.py:133
  103.9 1.8 %collective-permute-start.9 = (f32[96,1024]{1,0:T(8,128)S(1)}, f32[96,1024]{1,0:T(8,128)S(1)}, u32[]{:S(2)}, u32[]{:S(2)}) collective-permute-start(f32[96,1024]{1,0:T(8,128)S(1)} %pad_maximum_fusion), channel_id=1, source_target_pairs={{0,16},{1,17},{2,18},{3,19},{4,20},{5,21},{6,22},{7,23},{8,24},{9,... | collective-permute-start | bytes 1179656 | tf_op jit(solution)/shard_map/ppermute | solution.py:136

commit v2 on v1

v2 whole, which is shorter than its diff:
```python
import functools

import jax
import jax.numpy as jnp
from jax import lax
from jax.experimental import pallas as pl
from jax.experimental.pallas import tpu as pltpu
from jax.sharding import PartitionSpec as P

STEP = 1000
LANES = 128
SUBLANES = 8
AXES = ("section", "dp")
ROUNDS = ((0, 0), (2, 0), (0, 1), (2, 1), (1, 0), (3, 0), (1, 1), (3, 1))
PARAMS = pltpu.CompilerParams(vmem_limit_bytes=40 * 2**20)
ALONE = pltpu.CompilerParams(vmem_limit_bytes=62 * 2**20)


def target(old_section, block, shift, flip):
    z, core = old_section >> 1, old_section & 1
    y, x = block >> 2, block & 3
    turn = 2 * ((y + shift) & 3) + ((x & 1) ^ flip)
    odd = (z & 1) ^ core
    move = (turn + odd * (4 - 2 * turn)) * (1 - 2 * core)
    return 2 * ((z + move) & 7) + (core ^ (x >> 1))


def origin(old_section, new_section, shift, flip):
    z, core = old_section >> 1, old_section & 1
    move = ((new_section >> 1) - z) * (1 - 2 * core)
    odd = (z & 1) ^ core
    turn = (move + odd * (4 - 2 * move)) & 7
    y = ((turn >> 1) - shift) & 3
    x = 2 * (core ^ (new_section & 1)) + ((turn & 1) ^ flip)
    return 4 * y + x


def round_pairs(shift, flip):
    pairs = []
    for section in range(16):
        for rank in range(16):
            there = target(section, rank, shift, flip)
            pairs.append((section * 16 + rank, there * 16 + section))
    return pairs


SWAP = [(s * 16 + r, (s ^ 1) * 16 + r) for s in range(16) for r in range(16)]


def pack_kernel(slots, rounds, old_hbm, new_hbm, *refs):
    states, messages = refs[:3], refs[3 : 3 + len(rounds)]
    old_ref, new_ref, row_of, small_sem, state_sem = refs[3 + len(rounds) : 8 + len(rounds)]
    landed, tiles = refs[8 + len(rounds) : 11 + len(rounds)], refs[11 + len(rounds) :]
    section, rank = lax.axis_index("section"), lax.axis_index("dp")
    columns = states[0].shape[1] // LANES
    small = [
        pltpu.make_async_copy(old_hbm, old_ref, small_sem.at[0]),
        pltpu.make_async_copy(new_hbm, new_ref, small_sem.at[1]),
    ]
    large = []
    for index in range(3):
        for half in range(slots // SUBLANES):
            rows = pl.ds(half * SUBLANES, SUBLANES)
            large.append(
                pltpu.make_async_copy(
                    states[index].at[rows], landed[index].at[rows], state_sem.at[index, half]
                )
            )
    for copy in small + large:
        copy.start()
    for copy in small:
        copy.wait()
    for slot in range(slots):
        row_of[old_ref[section * slots + slot]] = slot
    for index in range(3):
        for half in range(slots // SUBLANES):
            large[index * (slots // SUBLANES) + half].wait()
            for column in range(columns):
                tiles[index][pl.ds((half * columns + column) * SUBLANES, SUBLANES), :] = landed[index][
                    pl.ds(half * SUBLANES, SUBLANES), pl.ds(column * LANES, LANES)
                ]
    for message, (shift, flip) in zip(messages, rounds):
        there = target(section, rank, shift, flip)
        for part in range(2):
            row = row_of[new_ref[(there ^ part) * slots + section]]
            start = (row >> 3) * (columns * SUBLANES) + (row & 7)
            for index, tile in enumerate(tiles):
                for half in range(2):
                    for column in range(8):
                        message[
                            pl.ds((part * 3 + index) * 16 + half * SUBLANES, SUBLANES),
                            pl.ds(column * LANES, LANES),
                        ] = tile[
                            pl.ds(start + (64 * half + column) * SUBLANES, SUBLANES, stride=64), :
                        ]


def pack(rounds, old_layers, new_layers, states):
    slots, columns = states[0].shape
    total = old_layers.shape[0]
    return pl.pallas_call(
        functools.partial(pack_kernel, slots, rounds),
        out_shape=[jax.ShapeDtypeStruct((96, 1024), jnp.float32)] * len(rounds),
        in_specs=[pl.BlockSpec(memory_space=pltpu.HBM)] * 5,
        out_specs=[pl.BlockSpec(memory_space=pltpu.VMEM)] * len(rounds),
        scratch_shapes=[pltpu.SMEM((total,), jnp.int32)] * 3
        + [pltpu.SemaphoreType.DMA((2,)), pltpu.SemaphoreType.DMA((3, slots // SUBLANES))]
        + [pltpu.VMEM((slots, columns), jnp.float32)] * 3
        + [pltpu.VMEM((slots * columns // LANES, LANES), jnp.float32)] * 3,
        compiler_params=ALONE,
        cost_estimate=pl.CostEstimate(flops=0, bytes_accessed=3 * 2**20, transcendentals=0),
    )(old_layers, new_layers, *states)


def adamw(weight, first, second, grad, live):
    first = 0.9 * first + 0.1 * grad
    second = 0.95 * second + 0.05 * grad * grad
    step_size = first / (1.0 - 0.9**STEP) / (jnp.sqrt(second / (1.0 - 0.95**STEP)) + 1e-08)
    weight = weight - 0.01 * (step_size + 0.1 * weight)
    zero = jnp.float32(0.0)
    return (
        jnp.where(live, weight, zero),
        jnp.where(live, first, zero),
        jnp.where(live, second, zero),
    )


def update_kernel(slots, rounds, packed, kept, counts_hbm, new_hbm, grads, *refs):
    count = 1 if packed else len(rounds)
    earlier = 0 if kept else 4
    held = refs[:count]
    outs = refs[count + earlier : count + earlier + 4]
    counts_ref, new_ref, small_sem, out_sem = refs[count + earlier + 4 : count + earlier + 8]
    done = refs[count + earlier + 8 :]
    section, rank = lax.axis_index("section"), lax.axis_index("dp")
    small = [
        pltpu.make_async_copy(counts_hbm, counts_ref, small_sem.at[0]),
        pltpu.make_async_copy(new_hbm, new_ref, small_sem.at[1]),
    ]
    for copy in small:
        copy.start()
    for copy in small:
        copy.wait()
    limit = counts_ref[new_ref[section * slots + rank]]
    width = grads.shape[1]
    place = width * lax.broadcasted_iota(jnp.int32, (16, width), 0) + lax.broadcasted_iota(
        jnp.int32, (16, width), 1
    )
    copies = []
    for number, (shift, flip) in enumerate(rounds):
        spot = origin(rank, section, shift, flip) ^ (0 if kept else 2)
        source = held[0].at[pl.ds(48 * number, 48)] if packed else held[number]
        rows = pl.ds(pl.multiple_of(spot * 16, 16), 16)
        live = place < limit - spot * (16 * width)
        results = adamw(
            source[pl.ds(0, 16), :], source[pl.ds(16, 16), :], source[pl.ds(32, 16), :], grads[rows, :], live
        )
        results = (*results, results[0].astype(jnp.bfloat16))
        for index, result in enumerate(results):
            done[index][pl.ds(number * 16, 16), :] = result
            copy = pltpu.make_async_copy(
                done[index].at[pl.ds(number * 16, 16)], outs[index].at[rows], out_sem.at[index, number]
            )
            copy.start()
            copies.append(copy)
    for copy in copies:
        copy.wait()


def update(rounds, counts, new_layers, grads, arrived, before):
    slots = 16
    hbm = pl.BlockSpec(memory_space=pltpu.HBM)
    vmem = pl.BlockSpec(memory_space=pltpu.VMEM)
    count = len(rounds)
    shapes = [jax.ShapeDtypeStruct(grads.shape, jnp.float32)] * 3 + [
        jax.ShapeDtypeStruct(grads.shape, jnp.bfloat16)
    ]
    return pl.pallas_call(
        functools.partial(update_kernel, slots, rounds, len(arrived) < count, not before),
        out_shape=shapes,
        in_specs=[hbm, hbm] + [vmem] * (len(arrived) + 1) + [hbm] * len(before),
        out_specs=[hbm] * 4,
        scratch_shapes=[pltpu.SMEM(counts.shape, jnp.int32)] * 2
        + [pltpu.SemaphoreType.DMA((2,)), pltpu.SemaphoreType.DMA((4, count))]
        + [pltpu.VMEM((16 * count, grads.shape[1]), shape.dtype) for shape in shapes],
        input_output_aliases={len(arrived) + 3 + i: i for i in range(len(before))},
        compiler_params=PARAMS,
        cost_estimate=pl.CostEstimate(
            flops=count * 2**20, bytes_accessed=count * 2**20, transcendentals=count * 2**16
        ),
    )(counts, new_layers, grads, *arrived, *before)


def on_device(master, momentum, variance, grads, counts, old_layers, new_layers):
    states = (master, momentum, variance)
    messages = pack(ROUNDS[:1], old_layers, new_layers, states) + pack(
        ROUNDS[1:], old_layers, new_layers, states
    )
    arrived = [
        lax.ppermute(message, AXES, round_pairs(*turn)) for message, turn in zip(messages, ROUNDS)
    ]
    swapped = lax.ppermute(jnp.concatenate([got[48:] for got in arrived]), AXES, SWAP)
    outs = update(ROUNDS, counts, new_layers, grads, arrived, ())
    return tuple(update(ROUNDS, counts, new_layers, grads, [swapped], outs))


def solution(mesh):
    placed = (
        P("section", "dp"),
        P("section", "dp"),
        P("section", "dp"),
        P(("section", "dp"), None),
        P(),
        P(),
        P(),
    )
    return jax.shard_map(
        on_device,
        mesh=mesh,
        in_specs=placed,
        out_specs=(
            P(("section", "dp"), None),
            P(("section", "dp"), None),
            P(("section", "dp"), None),
            P(("section", "dp"), None),
        ),
        check_vma=False,
    )
```

time: 110 us -> 98.7 us (0.90)
  the two profiles are of different devices: /device:TPU:23 before, /device:TPU:233 now
where the time goes in v2:
time: 98.7 us; the launch traced here: 98.4 us
  starting transfers between devices  51.5 us (52%)
  waiting for transfers between devices  34 us (34%)
  Pallas kernels  11.9 us (12%)
    ppermute x8, starting transfers between devices, on_device(): lax.ppermute(message, AXES, round_pairs(*turn))  51.4 us
    ppermute x8, waiting for transfers between devices, on_device(): lax.ppermute(message, AXES, round_pairs(*turn))  32.8 us
    pallas_call x2, Pallas kernels, pack(): pl.pallas_call(functools.partial(pack_kernel, slots, rounds), out_shape=[...  7.62 us
    pallas_call x2, Pallas kernels, update(): pl.pallas_call(functools.partial(update_kernel, slots, rounds, len(arrive...  4.27 us
  transfers between devices with their start and end apart: 9, of which 5 were waited for; matrix products, arithmetic and copies ran while one was open for 0% of the time, Pallas kernels for 7%

profile of v2, /device:TPU:233, one launch (start us, length us, event | category | flops | bytes accessed | tf_op | source)
XLA Modules:
  0.0 98.4 jit_solution(17329196898746062245)
XLA Ops:
  0.6 2.9 %shard_map.102 = f32[96,1024]{1,0:T(8,128)} custom-call(s32[256]{0:T(256)} %old_hbm.3, s32[256]{0:T(256)} %new_hbm.7, f32[16,16384]{1,0:T(8,128)} %refs_0_.3, f32[16,16384]{1,0:T(8,128)} %refs_1_.3, f32[16,16384]{1,0:T(8,128)} %refs_2_.3), custom_call_target="tpu_custom_call" | custom-call | bytes 3145728 | tf_op jit(solution)/shard_map/pallas_call | solution.py:101
  3.6 7.0 %collective-permute-start = (f32[96,1024]{1,0:T(8,128)}, f32[96,1024]{1,0:T(8,128)S(1)}, u32[]{:S(2)}, u32[]{:S(2)}) collective-permute-start(f32[96,1024]{1,0:T(8,128)} %shard_map.102), channel_id=1, source_target_pairs={{0,0},{1,32},{2,16},{3,48},{4,64},{5,96},{6,80},{7,112},{8,128},{9... | collective-permute-start | bytes 1179656 | tf_op jit(solution)/shard_map/ppermute | solution.py:200
  10.6 4.7 %shard_map.103 = (f32[96,1024]{1,0:T(8,128)}, f32[96,1024]{1,0:T(8,128)}, f32[96,1024]{1,0:T(8,128)}, f32[96,1024]{1,0:T(8,128)}, f32[96,1024]{1,0:T(8,128)}, /*index=5*/f32[96,1024]{1,0:T(8,128)}, f32[96,1024]{1,0:T(8,128)}) custom-call(s32[256]{0:T(256)} %old_hbm.3, s32[256]{0:T(256)} %new_hbm.7, f32[16,16384]{1,0:T(8,128)} %refs_0_.3, ...), custom_call_target="tpu_custom_call" | custom-call | bytes 3145728 | tf_op jit(solution)/shard_map/pallas_call | solution.py:101
  15.3 1.9 %collective-permute-start.1 = (f32[96,1024]{1,0:T(8,128)}, f32[96,1024]{1,0:T(8,128)S(1)}, u32[]{:S(2)}, u32[]{:S(2)}) collective-permute-start(f32[96,1024]{1,0:T(8,128)} %get-tuple-element.15), channel_id=1, source_target_pairs={{0,128},{1,160},{2,144},{3,176},{4,192},{5,224},{6,208},{7,240},{8... | collective-permute-start | bytes 1179656 | tf_op jit(solution)/shard_map/ppermute | solution.py:200
  17.2 5.6 %collective-permute-start.2 = (f32[96,1024]{1,0:T(8,128)}, f32[96,1024]{1,0:T(8,128)S(1)}, u32[]{:S(2)}, u32[]{:S(2)}) collective-permute-start(f32[96,1024]{1,0:T(8,128)} %get-tuple-element.16), channel_id=1, source_target_pairs={{0,32},{1,0},{2,48},{3,16},{4,96},{5,64},{6,112},{7,80},{8,160},{9... | collective-permute-start | bytes 1179656 | tf_op jit(solution)/shard_map/ppermute | solution.py:200
  22.8 7.1 %collective-permute-start.3 = (f32[96,1024]{1,0:T(8,128)}, f32[96,1024]{1,0:T(8,128)S(1)}, u32[]{:S(2)}, u32[]{:S(2)}) collective-permute-start(f32[96,1024]{1,0:T(8,128)} %get-tuple-element.17), channel_id=1, source_target_pairs={{0,160},{1,128},{2,176},{3,144},{4,224},{5,192},{6,240},{7,208},{8... | collective-permute-start | bytes 1179656 | tf_op jit(solution)/shard_map/ppermute | solution.py:200
  29.9 3.0 %collective-permute-start.4 = (f32[96,1024]{1,0:T(8,128)}, f32[96,1024]{1,0:T(8,128)S(1)}, u32[]{:S(2)}, u32[]{:S(2)}) collective-permute-start(f32[96,1024]{1,0:T(8,128)} %get-tuple-element.18), channel_id=1, source_target_pairs={{0,64},{1,96},{2,80},{3,112},{4,128},{5,160},{6,144},{7,176},{8,19... | collective-permute-start | bytes 1179656 | tf_op jit(solution)/shard_map/ppermute | solution.py:200
  32.8 0.0 collective-permute-done.refs_0_
  32.8 0.0 copy-start
  32.9 0.0 copy-start.1
  32.9 0.0 copy-start.2
  32.9 4.9 %collective-permute-start.5 = (f32[96,1024]{1,0:T(8,128)}, f32[96,1024]{1,0:T(8,128)S(1)}, u32[]{:S(2)}, u32[]{:S(2)}) collective-permute-start(f32[96,1024]{1,0:T(8,128)} %get-tuple-element.19), channel_id=1, source_target_pairs={{0,192},{1,224},{2,208},{3,240},{4,0},{5,32},{6,16},{7,48},{8,64},... | collective-permute-start | bytes 1179656 | tf_op jit(solution)/shard_map/ppermute | solution.py:200
  37.8 17.7 %collective-permute-done.1.refs_1_ = f32[96,1024]{1,0:T(8,128)S(1)} collective-permute-done((f32[96,1024]{1,0:T(8,128)}, f32[96,1024]{1,0:T(8,128)S(1)}, u32[]{:S(2)}, u32[]{:S(2)}) %collective-permute-start.1) | collective-permute-done | bytes 393248 | tf_op jit(solution)/shard_map/ppermute | solution.py:200
  55.5 20.1 %collective-permute-start.6 = (f32[96,1024]{1,0:T(8,128)}, f32[96,1024]{1,0:T(8,128)S(1)}, u32[]{:S(2)}, u32[]{:S(2)}) collective-permute-start(f32[96,1024]{1,0:T(8,128)} %get-tuple-element.20), channel_id=1, source_target_pairs={{0,96},{1,64},{2,112},{3,80},{4,160},{5,128},{6,176},{7,144},{8,22... | collective-permute-start | bytes 1179656 | tf_op jit(solution)/shard_map/ppermute | solution.py:200
  75.6 0.0 collective-permute-done.2.refs_2_
  75.6 1.9 %collective-permute-start.7 = (f32[96,1024]{1,0:T(8,128)}, f32[96,1024]{1,0:T(8,128)S(1)}, u32[]{:S(2)}, u32[]{:S(2)}) collective-permute-start(f32[96,1024]{1,0:T(8,128)} %get-tuple-element.21), channel_id=1, source_target_pairs={{0,224},{1,192},{2,240},{3,208},{4,32},{5,0},{6,48},{7,16},{8,96},... | collective-permute-start | bytes 1179656 | tf_op jit(solution)/shard_map/ppermute | solution.py:200
  77.5 0.0 collective-permute-done.3.refs_3_
  77.6 5.5 %collective-permute-done.4.refs_4_ = f32[96,1024]{1,0:T(8,128)S(1)} collective-permute-done((f32[96,1024]{1,0:T(8,128)}, f32[96,1024]{1,0:T(8,128)S(1)}, u32[]{:S(2)}, u32[]{:S(2)}) %collective-permute-start.4) | collective-permute-done | bytes 393248 | tf_op jit(solution)/shard_map/ppermute | solution.py:200
  83.1 0.0 collective-permute-done.5.refs_5_
  83.1 2.5 %collective-permute-done.6.refs_6_ = f32[96,1024]{1,0:T(8,128)S(1)} collective-permute-done((f32[96,1024]{1,0:T(8,128)}, f32[96,1024]{1,0:T(8,128)S(1)}, u32[]{:S(2)}, u32[]{:S(2)}) %collective-permute-start.6) | collective-permute-done | bytes 393248 | tf_op jit(solution)/shard_map/ppermute | solution.py:200
  85.7 7.0 %collective-permute-done.7.refs_7_ = f32[96,1024]{1,0:T(8,128)S(1)} collective-permute-done((f32[96,1024]{1,0:T(8,128)}, f32[96,1024]{1,0:T(8,128)S(1)}, u32[]{:S(2)}, u32[]{:S(2)}) %collective-permute-start.7) | collective-permute-done | bytes 393248 | tf_op jit(solution)/shard_map/ppermute | solution.py:200
  92.7 0.1 collective-permute-start.8
  92.8 0.0 copy-done
  92.8 0.0 copy-done.1
  92.8 0.0 copy-done.2
  92.9 2.1 %shard_map.104 = (f32[256,1024]{1,0:T(8,128)}, f32[256,1024]{1,0:T(8,128)}, f32[256,1024]{1,0:T(8,128)}, bf16[256,1024]{1,0:T(8,128)(2,1)}) custom-call(s32[256]{0:T(256)S(1)} %copy-done.2, s32[256]{0:T(256)S(1)} %copy-done.1, f32[256,1024]{1,0:T(8,128)S(1)} %copy-done, f32[96,1024]{1,0:T(8,128)S(1)} %collective-permute-done.refs_0_, ...), custom_call_target="tpu_custom_call" | custom-call | flops 8388608 | bytes 8388608 | tf_op jit(solution)/shard_map/pallas_call | solution.py:178
  95.0 1.2 %collective-permute-done.8.refs_0_ = f32[384,1024]{1,0:T(8,128)S(1)} collective-permute-done((f32[384,1024]{1,0:T(8,128)S(1)}, f32[384,1024]{1,0:T(8,128)S(1)}, u32[]{:S(2)}, u32[]{:S(2)}) %collective-permute-start.8) | collective-permute-done | bytes 1572896 | tf_op jit(solution)/shard_map/ppermute | solution.py:202
  96.2 2.1 %shard_map.105 = (f32[256,1024]{1,0:T(8,128)}, f32[256,1024]{1,0:T(8,128)}, f32[256,1024]{1,0:T(8,128)}, bf16[256,1024]{1,0:T(8,128)(2,1)}) custom-call(s32[256]{0:T(256)S(1)} %copy-done.2, s32[256]{0:T(256)S(1)} %copy-done.1, f32[256,1024]{1,0:T(8,128)S(1)} %copy-done, ...), custom_call_target="tpu_custom_call", output_to_operand_aliasing={{0}: (4, {}), {1}: (5, {}), {2}: (6, {}), {3}: (7, {})} | custom-call | flops 8388608 | bytes 8388608 | tf_op jit(solution)/shard_map/pallas_call | solution.py:178
  (8 shorter events, 0.1 us)
Async XLA Ops:
  3.6 29.3 %collective-permute-start = (f32[96,1024]{1,0:T(8,128)}, f32[96,1024]{1,0:T(8,128)S(1)}, u32[]{:S(2)}, u32[]{:S(2)}) collective-permute-start(f32[96,1024]{1,0:T(8,128)} %shard_map.102), channel_id=1, source_target_pairs={{0,0},{1,32},{2,16},{3,48},{4,64},{5,96},{6,80},{7,112},{8,128},{9... | collective-permute-start | bytes 1179656 | tf_op jit(solution)/shard_map/ppermute | solution.py:200
  15.3 40.2 %collective-permute-start.1 = (f32[96,1024]{1,0:T(8,128)}, f32[96,1024]{1,0:T(8,128)S(1)}, u32[]{:S(2)}, u32[]{:S(2)}) collective-permute-start(f32[96,1024]{1,0:T(8,128)} %get-tuple-element.15), channel_id=1, source_target_pairs={{0,128},{1,160},{2,144},{3,176},{4,192},{5,224},{6,208},{7,240},{8... | collective-permute-start | bytes 1179656 | tf_op jit(solution)/shard_map/ppermute | solution.py:200
  17.2 58.4 %collective-permute-start.2 = (f32[96,1024]{1,0:T(8,128)}, f32[96,1024]{1,0:T(8,128)S(1)}, u32[]{:S(2)}, u32[]{:S(2)}) collective-permute-start(f32[96,1024]{1,0:T(8,128)} %get-tuple-element.16), channel_id=1, source_target_pairs={{0,32},{1,0},{2,48},{3,16},{4,96},{5,64},{6,112},{7,80},{8,160},{9... | collective-permute-start | bytes 1179656 | tf_op jit(solution)/shard_map/ppermute | solution.py:200
  22.8 54.7 %collective-permute-start.3 = (f32[96,1024]{1,0:T(8,128)}, f32[96,1024]{1,0:T(8,128)S(1)}, u32[]{:S(2)}, u32[]{:S(2)}) collective-permute-start(f32[96,1024]{1,0:T(8,128)} %get-tuple-element.17), channel_id=1, source_target_pairs={{0,160},{1,128},{2,176},{3,144},{4,224},{5,192},{6,240},{7,208},{8... | collective-permute-start | bytes 1179656 | tf_op jit(solution)/shard_map/ppermute | solution.py:200
  29.9 53.2 %collective-permute-start.4 = (f32[96,1024]{1,0:T(8,128)}, f32[96,1024]{1,0:T(8,128)S(1)}, u32[]{:S(2)}, u32[]{:S(2)}) collective-permute-start(f32[96,1024]{1,0:T(8,128)} %get-tuple-element.18), channel_id=1, source_target_pairs={{0,64},{1,96},{2,80},{3,112},{4,128},{5,160},{6,144},{7,176},{8,19... | collective-permute-start | bytes 1179656 | tf_op jit(solution)/shard_map/ppermute | solution.py:200
  32.8 60.0 %copy-start = (f32[256,1024]{1,0:T(8,128)S(1)}, f32[256,1024]{1,0:T(8,128)}, u32[]{:S(2)}) copy-start(f32[256,1024]{1,0:T(8,128)} %grads.3) | copy-start | bytes 3145732
  32.9 60.0 %copy-start.1 = (s32[256]{0:T(256)S(1)}, s32[256]{0:T(256)}, u32[]{:S(2)}) copy-start(s32[256]{0:T(256)} %new_hbm.7) | copy-start | bytes 3076
  32.9 60.0 %copy-start.2 = (s32[256]{0:T(256)S(1)}, s32[256]{0:T(256)}, u32[]{:S(2)}) copy-start(s32[256]{0:T(256)} %counts_hbm.3) | copy-start | bytes 3076
  32.9 50.2 %collective-permute-start.5 = (f32[96,1024]{1,0:T(8,128)}, f32[96,1024]{1,0:T(8,128)S(1)}, u32[]{:S(2)}, u32[]{:S(2)}) collective-permute-start(f32[96,1024]{1,0:T(8,128)} %get-tuple-element.19), channel_id=1, source_target_pairs={{0,192},{1,224},{2,208},{3,240},{4,0},{5,32},{6,16},{7,48},{8,64},... | collective-permute-start | bytes 1179656 | tf_op jit(solution)/shard_map/ppermute | solution.py:200
  55.5 30.2 %collective-permute-start.6 = (f32[96,1024]{1,0:T(8,128)}, f32[96,1024]{1,0:T(8,128)S(1)}, u32[]{:S(2)}, u32[]{:S(2)}) collective-permute-start(f32[96,1024]{1,0:T(8,128)} %get-tuple-element.20), channel_id=1, source_target_pairs={{0,96},{1,64},{2,112},{3,80},{4,160},{5,128},{6,176},{7,144},{8,22... | collective-permute-start | bytes 1179656 | tf_op jit(solution)/shard_map/ppermute | solution.py:200
  75.6 17.1 %collective-permute-start.7 = (f32[96,1024]{1,0:T(8,128)}, f32[96,1024]{1,0:T(8,128)S(1)}, u32[]{:S(2)}, u32[]{:S(2)}) collective-permute-start(f32[96,1024]{1,0:T(8,128)} %get-tuple-element.21), channel_id=1, source_target_pairs={{0,224},{1,192},{2,240},{3,208},{4,32},{5,0},{6,48},{7,16},{8,96},... | collective-permute-start | bytes 1179656 | tf_op jit(solution)/shard_map/ppermute | solution.py:200
  92.7 3.5 %collective-permute-start.8 = (f32[384,1024]{1,0:T(8,128)S(1)}, f32[384,1024]{1,0:T(8,128)S(1)}, u32[]{:S(2)}, u32[]{:S(2)}) collective-permute-start(f32[384,1024]{1,0:T(8,128)S(1)} %slice_dynamic-update-slice_fusion), channel_id=1, source_target_pairs={{0,16},{1,17},{2,18},{3,19},{4,20},{5,21},{6,22},{7,23},{8,24},{9,... | collective-permute-start | bytes 4718600 | tf_op jit(solution)/shard_map/ppermute | solution.py:202

commit v3 on v2

--- a/solution.py
+++ b/solution.py
@@ -11,7 +11,10 @@
 LANES = 128
 SUBLANES = 8
 AXES = ("section", "dp")
-ROUNDS = ((0, 0), (2, 0), (0, 1), (2, 1), (1, 0), (3, 0), (1, 1), (3, 1))
+PACKS = ((0, 1), (2, 3, 4, 5, 6, 7))
+SWAPS = ((0, 1), (2, 3), (4, 5), (6,), (7,))
+UPDATES = (((0, 1, 2, 3, 4, 5), (0, 1, 2)), ((6, 7), (3, 4)))
+ROUNDS = ((0, 0), (2, 0), (1, 1), (3, 1), (1, 0), (3, 0), (0, 1), (2, 1))
 PARAMS = pltpu.CompilerParams(vmem_limit_bytes=40 * 2**20)
 ALONE = pltpu.CompilerParams(vmem_limit_bytes=62 * 2**20)
 
@@ -49,8 +52,8 @@
 
 def pack_kernel(slots, rounds, old_hbm, new_hbm, *refs):
     states, messages = refs[:3], refs[3 : 3 + len(rounds)]
-    old_ref, new_ref, row_of, small_sem, state_sem = refs[3 + len(rounds) : 8 + len(rounds)]
-    landed, tiles = refs[8 + len(rounds) : 11 + len(rounds)], refs[11 + len(rounds) :]
+    old_ref, new_ref, row_of, small_sem, state_sem, out_sem, filled = refs[3 + len(rounds) : 10 + len(rounds)]
+    landed, tiles = refs[10 + len(rounds) : 13 + len(rounds)], refs[13 + len(rounds) :]
     section, rank = lax.axis_index("section"), lax.axis_index("dp")
     columns = states[0].shape[1] // LANES
     small = [
@@ -79,7 +82,9 @@
                 tiles[index][pl.ds((half * columns + column) * SUBLANES, SUBLANES), :] = landed[index][
                     pl.ds(half * SUBLANES, SUBLANES), pl.ds(column * LANES, LANES)
                 ]
-    for message, (shift, flip) in zip(messages, rounds):
+    copies = []
+    for number, (shift, flip) in enumerate(rounds):
+        message = filled.at[number]
         there = target(section, rank, shift, flip)
         for part in range(2):
             row = row_of[new_ref[(there ^ part) * slots + section]]
@@ -93,6 +98,11 @@
                         ] = tile[
                             pl.ds(start + (64 * half + column) * SUBLANES, SUBLANES, stride=64), :
                         ]
+        copy = pltpu.make_async_copy(message, messages[number], out_sem.at[number])
+        copy.start()
+        copies.append(copy)
+    for copy in copies:
+        copy.wait()
 
 
 def pack(rounds, old_layers, new_layers, states):
@@ -102,9 +112,10 @@
         functools.partial(pack_kernel, slots, rounds),
         out_shape=[jax.ShapeDtypeStruct((96, 1024), jnp.float32)] * len(rounds),
         in_specs=[pl.BlockSpec(memory_space=pltpu.HBM)] * 5,
-        out_specs=[pl.BlockSpec(memory_space=pltpu.VMEM)] * len(rounds),
+        out_specs=[pl.BlockSpec(memory_space=pltpu.HBM)] * len(rounds),
         scratch_shapes=[pltpu.SMEM((total,), jnp.int32)] * 3
         + [pltpu.SemaphoreType.DMA((2,)), pltpu.SemaphoreType.DMA((3, slots // SUBLANES))]
+        + [pltpu.SemaphoreType.DMA((len(rounds),)), pltpu.VMEM((len(rounds), 96, 1024), jnp.float32)]
         + [pltpu.VMEM((slots, columns), jnp.float32)] * 3
         + [pltpu.VMEM((slots * columns // LANES, LANES), jnp.float32)] * 3,
         compiler_params=ALONE,
@@ -125,13 +136,11 @@
     )
 
 
-def update_kernel(slots, rounds, packed, kept, counts_hbm, new_hbm, grads, *refs):
-    count = 1 if packed else len(rounds)
-    earlier = 0 if kept else 4
-    held = refs[:count]
-    outs = refs[count + earlier : count + earlier + 4]
-    counts_ref, new_ref, small_sem, out_sem = refs[count + earlier + 4 : count + earlier + 8]
-    done = refs[count + earlier + 8 :]
+def update_kernel(slots, pieces, arrays, earlier, counts_hbm, new_hbm, grads, *refs):
+    held = refs[:arrays]
+    outs = refs[arrays + earlier : arrays + earlier + 4]
+    counts_ref, new_ref, small_sem, out_sem = refs[arrays + earlier + 4 : arrays + earlier + 8]
+    done = refs[arrays + earlier + 8 :]
     section, rank = lax.axis_index("section"), lax.axis_index("dp")
     small = [
         pltpu.make_async_copy(counts_hbm, counts_ref, small_sem.at[0]),
@@ -147,9 +156,9 @@
         jnp.int32, (16, width), 1
     )
     copies = []
-    for number, (shift, flip) in enumerate(rounds):
-        spot = origin(rank, section, shift, flip) ^ (0 if kept else 2)
-        source = held[0].at[pl.ds(48 * number, 48)] if packed else held[number]
+    for number, (array, offset, turn, kept) in enumerate(pieces):
+        spot = origin(rank, section, *ROUNDS[turn]) ^ (0 if kept else 2)
+        source = held[array].at[pl.ds(offset, 48)]
         rows = pl.ds(pl.multiple_of(spot * 16, 16), 16)
         live = place < limit - spot * (16 * width)
         results = adamw(
@@ -167,41 +176,56 @@
         copy.wait()
 
 
-def update(rounds, counts, new_layers, grads, arrived, before):
+def update(kept, swapped, counts, new_layers, grads, arrived, exchanged, before):
     slots = 16
+    arrays, pieces = [], []
+    for turn in kept:
+        pieces.append((len(arrays), 0, turn, True))
+        arrays.append(arrived[turn])
+    for group in swapped:
+        for number, turn in enumerate(SWAPS[group]):
+            pieces.append((len(arrays), 48 * number, turn, False))
+        arrays.append(exchanged[group])
+    count = len(pieces)
     hbm = pl.BlockSpec(memory_space=pltpu.HBM)
     vmem = pl.BlockSpec(memory_space=pltpu.VMEM)
-    count = len(rounds)
     shapes = [jax.ShapeDtypeStruct(grads.shape, jnp.float32)] * 3 + [
         jax.ShapeDtypeStruct(grads.shape, jnp.bfloat16)
     ]
     return pl.pallas_call(
-        functools.partial(update_kernel, slots, rounds, len(arrived) < count, not before),
+        functools.partial(update_kernel, slots, tuple(pieces), len(arrays), len(before)),
         out_shape=shapes,
-        in_specs=[hbm, hbm] + [vmem] * (len(arrived) + 1) + [hbm] * len(before),
+        in_specs=[hbm, hbm] + [vmem] * (len(arrays) + 1) + [hbm] * len(before),
         out_specs=[hbm] * 4,
         scratch_shapes=[pltpu.SMEM(counts.shape, jnp.int32)] * 2
         + [pltpu.SemaphoreType.DMA((2,)), pltpu.SemaphoreType.DMA((4, count))]
         + [pltpu.VMEM((16 * count, grads.shape[1]), shape.dtype) for shape in shapes],
-        input_output_aliases={len(arrived) + 3 + i: i for i in range(len(before))},
+        input_output_aliases={len(arrays) + 3 + i: i for i in range(len(before))},
         compiler_params=PARAMS,
         cost_estimate=pl.CostEstimate(
-            flops=count * 2**20, bytes_accessed=count * 2**20, transcendentals=count * 2**16
+            flops=count * 2**20, bytes_accessed=count * 2**19, transcendentals=count * 2**16
         ),
-    )(counts, new_layers, grads, *arrived, *before)
+    )(counts, new_layers, grads, *arrays, *before)
 
 
 def on_device(master, momentum, variance, grads, counts, old_layers, new_layers):
     states = (master, momentum, variance)
-    messages = pack(ROUNDS[:1], old_layers, new_layers, states) + pack(
-        ROUNDS[1:], old_layers, new_layers, states
-    )
+    messages = []
+    for part in PACKS:
+        if messages:
+            old_layers, messages[-1] = lax.optimization_barrier((old_layers, messages[-1]))
+        messages += pack(tuple(ROUNDS[turn] for turn in part), old_layers, new_layers, states)
     arrived = [
         lax.ppermute(message, AXES, round_pairs(*turn)) for message, turn in zip(messages, ROUNDS)
     ]
-    swapped = lax.ppermute(jnp.concatenate([got[48:] for got in arrived]), AXES, SWAP)
-    outs = update(ROUNDS, counts, new_layers, grads, arrived, ())
-    return tuple(update(ROUNDS, counts, new_layers, grads, [swapped], outs))
+    exchanged = [
+        lax.ppermute(jnp.concatenate([arrived[turn][48:] for turn in group]), AXES, SWAP)
+        for group in SWAPS
+    ]
+    outs = ()
+    for kept, swapped in UPDATES:
+        outs = update(kept, swapped, counts, new_layers, grads, arrived, exchanged, outs)
+    return tuple(outs)
 
 
 def solution(mesh):

time: 98.7 us -> 93.9 us (0.951)
  the two profiles are of different devices: /device:TPU:233 before, /device:TPU:89 now
where the time goes in v3:
time: 93.9 us; the launch traced here: 93.5 us
  starting transfers between devices  56.9 us (61%)
  waiting for transfers between devices  23.8 us (25%)
  Pallas kernels  11.6 us (12%)
  between operations  1.03 us (1%)
    ppermute x8, starting transfers between devices, on_device(): lax.ppermute(message, AXES, round_pairs(*turn))  48.8 us
    ppermute x8, waiting for transfers between devices, on_device(): lax.ppermute(message, AXES, round_pairs(*turn))  23.8 us
    ppermute x5, starting transfers between devices, on_device(): lax.ppermute(jnp.concatenate([arrived[turn][48:] for turn in group]), AXE...  8.04 us
    pallas_call x2, Pallas kernels, pack(): pl.pallas_call(functools.partial(pack_kernel, slots, rounds), out_shape=[...  7.31 us
    pallas_call x2, Pallas kernels, update(): pl.pallas_call(functools.partial(update_kernel, slots, tuple(pieces), len...  4.27 us
  transfers between devices with their start and end apart: 13, of which 3 were waited for; matrix products, arithmetic and copies ran while one was open for 0% of the time, Pallas kernels for 7%

profile of v3, /device:TPU:89, one launch (start us, length us, event | category | flops | bytes accessed | tf_op | source)
XLA Modules:
  0.0 93.5 jit_solution(10457788135639342836)
XLA Ops:
  0.6 3.2 %shard_map.102 = (f32[96,1024]{1,0:T(8,128)}, f32[96,1024]{1,0:T(8,128)}) custom-call(s32[256]{0:T(256)} %old_hbm.2, s32[256]{0:T(256)} %new_hbm.7, f32[16,16384]{1,0:T(8,128)} %refs_0_.3, f32[16,16384]{1,0:T(8,128)} %refs_1_.3, f32[16,16384]{1,0:T(8,128)} %refs_2_.3), custom_call_target="tpu_custom_call" | custom-call | bytes 3145728 | tf_op jit(solution)/shard_map/pallas_call | solution.py:111
  3.8 2.9 %collective-permute-start.5 = (f32[96,1024]{1,0:T(8,128)}, f32[96,1024]{1,0:T(8,128)S(1)}, u32[]{:S(2)}, u32[]{:S(2)}) collective-permute-start(f32[96,1024]{1,0:T(8,128)} %get-tuple-element.23), channel_id=1, source_target_pairs={{0,128},{1,160},{2,144},{3,176},{4,192},{5,224},{6,208},{7,240},{8... | collective-permute-start | bytes 1179656 | tf_op jit(solution)/shard_map/ppermute | solution.py:219
  6.7 9.4 %collective-permute-start.4 = (f32[96,1024]{1,0:T(8,128)}, f32[96,1024]{1,0:T(8,128)S(1)}, u32[]{:S(2)}, u32[]{:S(2)}) collective-permute-start(f32[96,1024]{1,0:T(8,128)} %get-tuple-element.22), channel_id=1, source_target_pairs={{0,0},{1,32},{2,16},{3,48},{4,64},{5,96},{6,80},{7,112},{8,128},{9... | collective-permute-start | bytes 1179656 | tf_op jit(solution)/shard_map/ppermute | solution.py:219
  16.1 4.1 %shard_map.103 = (f32[96,1024]{1,0:T(8,128)}, f32[96,1024]{1,0:T(8,128)}, f32[96,1024]{1,0:T(8,128)}, f32[96,1024]{1,0:T(8,128)}, f32[96,1024]{1,0:T(8,128)}, /*index=5*/f32[96,1024]{1,0:T(8,128)}) custom-call(s32[256]{0:T(256)} %old_hbm.2, s32[256]{0:T(256)} %new_hbm.7, f32[16,16384]{1,0:T(8,128)} %refs_0_.3, f32[16,16384]{1,0:T(8,128)} %refs_1_.3, ...), custom_call_target="tpu_custom_call" | custom-call | bytes 3145728 | tf_op jit(solution)/shard_map/pallas_call | solution.py:111
  20.3 6.2 %collective-permute-start.6 = (f32[96,1024]{1,0:T(8,128)}, f32[96,1024]{1,0:T(8,128)S(1)}, u32[]{:S(2)}, u32[]{:S(2)}) collective-permute-start(f32[96,1024]{1,0:T(8,128)} %get-tuple-element.24), channel_id=1, source_target_pairs={{0,96},{1,64},{2,112},{3,80},{4,160},{5,128},{6,176},{7,144},{8,22... | collective-permute-start | bytes 1179656 | tf_op jit(solution)/shard_map/ppermute | solution.py:219
  26.4 3.7 %collective-permute-start.7 = (f32[96,1024]{1,0:T(8,128)}, f32[96,1024]{1,0:T(8,128)S(1)}, u32[]{:S(2)}, u32[]{:S(2)}) collective-permute-start(f32[96,1024]{1,0:T(8,128)} %get-tuple-element.25), channel_id=1, source_target_pairs={{0,224},{1,192},{2,240},{3,208},{4,32},{5,0},{6,48},{7,16},{8,96},... | collective-permute-start | bytes 1179656 | tf_op jit(solution)/shard_map/ppermute | solution.py:219
  30.1 6.0 %collective-permute-start.8 = (f32[96,1024]{1,0:T(8,128)}, f32[96,1024]{1,0:T(8,128)S(1)}, u32[]{:S(2)}, u32[]{:S(2)}) collective-permute-start(f32[96,1024]{1,0:T(8,128)} %get-tuple-element.26), channel_id=1, source_target_pairs={{0,64},{1,96},{2,80},{3,112},{4,128},{5,160},{6,144},{7,176},{8,19... | collective-permute-start | bytes 1179656 | tf_op jit(solution)/shard_map/ppermute | solution.py:219
  36.2 0.0 collective-permute-done.5.refs_1_
  36.2 2.1 %collective-permute-start.9 = (f32[96,1024]{1,0:T(8,128)}, f32[96,1024]{1,0:T(8,128)S(1)}, u32[]{:S(2)}, u32[]{:S(2)}) collective-permute-start(f32[96,1024]{1,0:T(8,128)} %get-tuple-element.27), channel_id=1, source_target_pairs={{0,192},{1,224},{2,208},{3,240},{4,0},{5,32},{6,16},{7,48},{8,64},... | collective-permute-start | bytes 1179656 | tf_op jit(solution)/shard_map/ppermute | solution.py:219
  38.3 6.6 %collective-permute-start = (f32[96,1024]{1,0:T(8,128)S(1)}, f32[96,1024]{1,0:T(8,128)S(1)}, u32[]{:S(2)}, u32[]{:S(2)}) collective-permute-start(f32[96,1024]{1,0:T(8,128)S(1)} %copy-done.10), channel_id=1, source_target_pairs={{0,32},{1,0},{2,48},{3,16},{4,96},{5,64},{6,112},{7,80},{8,160},{9... | collective-permute-start | bytes 1179656 | tf_op jit(solution)/shard_map/ppermute | solution.py:219
  45.0 0.0 collective-permute-done.6.refs_2_
  45.0 0.0 copy-start.5
  45.0 0.0 slice-start.1
  45.0 12.0 %collective-permute-start.1 = (f32[96,1024]{1,0:T(8,128)S(1)}, f32[96,1024]{1,0:T(8,128)S(1)}, u32[]{:S(2)}, u32[]{:S(2)}) collective-permute-start(f32[96,1024]{1,0:T(8,128)S(1)} %copy-done.9), channel_id=1, source_target_pairs={{0,160},{1,128},{2,176},{3,144},{4,224},{5,192},{6,240},{7,208},{8... | collective-permute-start | bytes 1179656 | tf_op jit(solution)/shard_map/ppermute | solution.py:219
  57.1 0.0 slice-start.2
  57.1 4.1 %collective-permute-done.7.refs_3_ = f32[96,1024]{1,0:T(8,128)S(1)} collective-permute-done((f32[96,1024]{1,0:T(8,128)}, f32[96,1024]{1,0:T(8,128)S(1)}, u32[]{:S(2)}, u32[]{:S(2)}) %collective-permute-start.7) | collective-permute-done | bytes 393248 | tf_op jit(solution)/shard_map/ppermute | solution.py:219
  61.2 0.0 collective-permute-start.10
  61.3 17.1 %collective-permute-done.8.refs_4_ = f32[96,1024]{1,0:T(8,128)S(1)} collective-permute-done((f32[96,1024]{1,0:T(8,128)}, f32[96,1024]{1,0:T(8,128)S(1)}, u32[]{:S(2)}, u32[]{:S(2)}) %collective-permute-start.8) | collective-permute-done | bytes 393248 | tf_op jit(solution)/shard_map/ppermute | solution.py:219
  78.4 0.0 collective-permute-start.11
  78.4 0.0 copy-start
  78.4 0.0 collective-permute-done.9.refs_5_
  78.4 0.0 copy-start.7
  78.5 0.0 copy-start.8
  78.5 0.6 collective-permute-start.12
  79.1 0.0 collective-permute-done.refs_0_
  79.1 5.4 %collective-permute-start.2 = (f32[48,1024]{1,0:T(8,128)S(1)}, f32[48,1024]{1,0:T(8,128)S(1)}, u32[]{:S(2)}, u32[]{:S(2)}) collective-permute-start(f32[48,1024]{1,0:T(8,128)S(1)} %slice.32), channel_id=1, source_target_pairs={{0,16},{1,17},{2,18},{3,19},{4,20},{5,21},{6,22},{7,23},{8,24},{9,... | collective-permute-start | bytes 589832 | tf_op jit(solution)/shard_map/ppermute | solution.py:222
  84.5 2.5 %collective-permute-done.1.refs_1_ = f32[96,1024]{1,0:T(8,128)S(1)} collective-permute-done((f32[96,1024]{1,0:T(8,128)S(1)}, f32[96,1024]{1,0:T(8,128)S(1)}, u32[]{:S(2)}, u32[]{:S(2)}) %collective-permute-start.1) | collective-permute-done | bytes 393248 | tf_op jit(solution)/shard_map/ppermute | solution.py:219
  87.1 2.1 %collective-permute-start.3 = (f32[48,1024]{1,0:T(8,128)S(1)}, f32[48,1024]{1,0:T(8,128)S(1)}, u32[]{:S(2)}, u32[]{:S(2)}) collective-permute-start(f32[48,1024]{1,0:T(8,128)S(1)} %slice.33), channel_id=1, source_target_pairs={{0,16},{1,17},{2,18},{3,19},{4,20},{5,21},{6,22},{7,23},{8,24},{9,... | collective-permute-start | bytes 589832 | tf_op jit(solution)/shard_map/ppermute | solution.py:222
  89.1 0.0 collective-permute-done.10.refs_6_
  89.2 2.6 %shard_map.104 = (f32[256,1024]{1,0:T(8,128)}, f32[256,1024]{1,0:T(8,128)}, f32[256,1024]{1,0:T(8,128)}, bf16[256,1024]{1,0:T(8,128)(2,1)}) custom-call(s32[256]{0:T(256)S(1)} %copy-done.8, s32[256]{0:T(256)S(1)} %copy-done.7, f32[256,1024]{1,0:T(8,128)S(1)} %copy-done, f32[96,1024]{1,0:T(8,128)S(1)} %copy-done.4, f32[96,1024]{1,0:T(8,128)S(1)} %copy-done.2, ...), custom_call_target="tpu_custom_call" | custom-call | flops 12582912 | bytes 6291456 | tf_op jit(solution)/shard_map/pallas_call | solution.py:195
  91.8 0.0 collective-permute-done.2.refs_2_
  91.8 1.7 %shard_map.105 = (f32[256,1024]{1,0:T(8,128)}, f32[256,1024]{1,0:T(8,128)}, f32[256,1024]{1,0:T(8,128)}, bf16[256,1024]{1,0:T(8,128)(2,1)}) custom-call(s32[256]{0:T(256)S(1)} %copy-done.8, s32[256]{0:T(256)S(1)} %copy-done.7, f32[256,1024]{1,0:T(8,128)S(1)} %copy-done, ...), custom_call_target="tpu_custom_call", output_to_operand_aliasing={{0}: (7, {}), {1}: (8, {}), {2}: (9, {}), {3}: (10, {})} | custom-call | flops 4194304 | bytes 2097152 | tf_op jit(solution)/shard_map/pallas_call | solution.py:195
  (34 shorter events, 0.2 us)
Async XLA Ops:
  3.8 32.4 %collective-permute-start.5 = (f32[96,1024]{1,0:T(8,128)}, f32[96,1024]{1,0:T(8,128)S(1)}, u32[]{:S(2)}, u32[]{:S(2)}) collective-permute-start(f32[96,1024]{1,0:T(8,128)} %get-tuple-element.23), channel_id=1, source_target_pairs={{0,128},{1,160},{2,144},{3,176},{4,192},{5,224},{6,208},{7,240},{8... | collective-permute-start | bytes 1179656 | tf_op jit(solution)/shard_map/ppermute | solution.py:219
  6.7 31.6 %collective-permute-start.4 = (f32[96,1024]{1,0:T(8,128)}, f32[96,1024]{1,0:T(8,128)S(1)}, u32[]{:S(2)}, u32[]{:S(2)}) collective-permute-start(f32[96,1024]{1,0:T(8,128)} %get-tuple-element.22), channel_id=1, source_target_pairs={{0,0},{1,32},{2,16},{3,48},{4,64},{5,96},{6,80},{7,112},{8,128},{9... | collective-permute-start | bytes 1179656 | tf_op jit(solution)/shard_map/ppermute | solution.py:219
  20.2 18.1 %copy-start.10 = (f32[96,1024]{1,0:T(8,128)S(1)}, f32[96,1024]{1,0:T(8,128)}, u32[]{:S(2)}) copy-start(f32[96,1024]{1,0:T(8,128)} %get-tuple-element.20) | copy-start | bytes 1179652
  20.3 24.7 %collective-permute-start.6 = (f32[96,1024]{1,0:T(8,128)}, f32[96,1024]{1,0:T(8,128)S(1)}, u32[]{:S(2)}, u32[]{:S(2)}) collective-permute-start(f32[96,1024]{1,0:T(8,128)} %get-tuple-element.24), channel_id=1, source_target_pairs={{0,96},{1,64},{2,112},{3,80},{4,160},{5,128},{6,176},{7,144},{8,22... | collective-permute-start | bytes 1179656 | tf_op jit(solution)/shard_map/ppermute | solution.py:219
  26.4 34.8 %collective-permute-start.7 = (f32[96,1024]{1,0:T(8,128)}, f32[96,1024]{1,0:T(8,128)S(1)}, u32[]{:S(2)}, u32[]{:S(2)}) collective-permute-start(f32[96,1024]{1,0:T(8,128)} %get-tuple-element.25), channel_id=1, source_target_pairs={{0,224},{1,192},{2,240},{3,208},{4,32},{5,0},{6,48},{7,16},{8,96},... | collective-permute-start | bytes 1179656 | tf_op jit(solution)/shard_map/ppermute | solution.py:219
  30.1 48.2 %collective-permute-start.8 = (f32[96,1024]{1,0:T(8,128)}, f32[96,1024]{1,0:T(8,128)S(1)}, u32[]{:S(2)}, u32[]{:S(2)}) collective-permute-start(f32[96,1024]{1,0:T(8,128)} %get-tuple-element.26), channel_id=1, source_target_pairs={{0,64},{1,96},{2,80},{3,112},{4,128},{5,160},{6,144},{7,176},{8,19... | collective-permute-start | bytes 1179656 | tf_op jit(solution)/shard_map/ppermute | solution.py:219
  36.2 2.1 %copy-start.1 = (f32[96,1024]{1,0:T(8,128)}, f32[96,1024]{1,0:T(8,128)S(1)}, u32[]{:S(2)}) copy-start(f32[96,1024]{1,0:T(8,128)S(1)} %collective-permute-done.5.refs_1_) | copy-start | bytes 1179652
  36.2 8.8 %copy-start.9 = (f32[96,1024]{1,0:T(8,128)S(1)}, f32[96,1024]{1,0:T(8,128)}, u32[]{:S(2)}) copy-start(f32[96,1024]{1,0:T(8,128)} %get-tuple-element.21) | copy-start | bytes 1179652
  36.2 42.2 %collective-permute-start.9 = (f32[96,1024]{1,0:T(8,128)}, f32[96,1024]{1,0:T(8,128)S(1)}, u32[]{:S(2)}, u32[]{:S(2)}) collective-permute-start(f32[96,1024]{1,0:T(8,128)} %get-tuple-element.27), channel_id=1, source_target_pairs={{0,192},{1,224},{2,208},{3,240},{4,0},{5,32},{6,16},{7,48},{8,64},... | collective-permute-start | bytes 1179656 | tf_op jit(solution)/shard_map/ppermute | solution.py:219
  38.3 6.7 %copy-start.3 = (f32[96,1024]{1,0:T(8,128)}, f32[96,1024]{1,0:T(8,128)S(1)}, u32[]{:S(2)}) copy-start(f32[96,1024]{1,0:T(8,128)S(1)} %collective-permute-done.4.refs_0_) | copy-start | bytes 1179652
  38.3 40.8 %collective-permute-start = (f32[96,1024]{1,0:T(8,128)S(1)}, f32[96,1024]{1,0:T(8,128)S(1)}, u32[]{:S(2)}, u32[]{:S(2)}) collective-permute-start(f32[96,1024]{1,0:T(8,128)S(1)} %copy-done.10), channel_id=1, source_target_pairs={{0,32},{1,0},{2,48},{3,16},{4,96},{5,64},{6,112},{7,80},{8,160},{9... | collective-permute-start | bytes 1179656 | tf_op jit(solution)/shard_map/ppermute | solution.py:219
  45.0 12.0 %copy-start.5 = (f32[96,1024]{1,0:T(8,128)}, f32[96,1024]{1,0:T(8,128)S(1)}, u32[]{:S(2)}) copy-start(f32[96,1024]{1,0:T(8,128)S(1)} %collective-permute-done.6.refs_2_) | copy-start | bytes 1179652
  45.0 12.0 %slice-start = ((f32[96,1024]{1,0:T(8,128)}), f32[48,1024]{1,0:T(8,128)S(1)}, s32[]{:S(2)}) async-start(f32[96,1024]{1,0:T(8,128)} %copy-done.1), calls=%async_computation | async-start | bytes 393216 | tf_op jit(solution)/shard_map/slice | solution.py:222
  45.0 12.0 %slice-start.1 = ((f32[96,1024]{1,0:T(8,128)}), f32[48,1024]{1,0:T(8,128)S(1)}, s32[]{:S(2)}) async-start(f32[96,1024]{1,0:T(8,128)} %copy-done.3), calls=%async_computation.1 | async-start | bytes 393216 | tf_op jit(solution)/shard_map/slice | solution.py:222
  45.0 42.0 %collective-permute-start.1 = (f32[96,1024]{1,0:T(8,128)S(1)}, f32[96,1024]{1,0:T(8,128)S(1)}, u32[]{:S(2)}, u32[]{:S(2)}) collective-permute-start(f32[96,1024]{1,0:T(8,128)S(1)} %copy-done.9), channel_id=1, source_target_pairs={{0,160},{1,128},{2,176},{3,144},{4,224},{5,192},{6,240},{7,208},{8... | collective-permute-start | bytes 1179656 | tf_op jit(solution)/shard_map/ppermute | solution.py:219
  57.1 4.2 %slice-start.2 = ((f32[96,1024]{1,0:T(8,128)}), f32[48,1024]{1,0:T(8,128)S(1)}, s32[]{:S(2)}) async-start(f32[96,1024]{1,0:T(8,128)} %copy-done.5), calls=%async_computation.2 | async-start | bytes 393216 | tf_op jit(solution)/shard_map/slice | solution.py:222
  61.2 27.9 %collective-permute-start.10 = (f32[96,1024]{1,0:T(8,128)S(1)}, f32[96,1024]{1,0:T(8,128)S(1)}, u32[]{:S(2)}, u32[]{:S(2)}) collective-permute-start(f32[96,1024]{1,0:T(8,128)S(1)} %pad_maximum_fusion), channel_id=1, source_target_pairs={{0,16},{1,17},{2,18},{3,19},{4,20},{5,21},{6,22},{7,23},{8,24},{9,... | collective-permute-start | bytes 1179656 | tf_op jit(solution)/shard_map/ppermute | solution.py:222
  78.4 10.8 %collective-permute-start.11 = (f32[96,1024]{1,0:T(8,128)S(1)}, f32[96,1024]{1,0:T(8,128)S(1)}, u32[]{:S(2)}, u32[]{:S(2)}) collective-permute-start(f32[96,1024]{1,0:T(8,128)S(1)} %pad_maximum_fusion.1), channel_id=1, source_target_pairs={{0,16},{1,17},{2,18},{3,19},{4,20},{5,21},{6,22},{7,23},{8,24},{9,... | collective-permute-start | bytes 1179656 | tf_op jit(solution)/shard_map/ppermute | solution.py:222
  78.4 10.8 %copy-start.6 = (f32[96,1024]{1,0:T(8,128)S(1)}, f32[96,1024]{1,0:T(8,128)}, u32[]{:S(2)}) copy-start(f32[96,1024]{1,0:T(8,128)} %copy-done.5) | copy-start | bytes 1179652
  78.4 10.8 %copy-start = (f32[256,1024]{1,0:T(8,128)S(1)}, f32[256,1024]{1,0:T(8,128)}, u32[]{:S(2)}) copy-start(f32[256,1024]{1,0:T(8,128)} %grads.3) | copy-start | bytes 3145732
  78.4 10.7 %copy-start.7 = (s32[256]{0:T(256)S(1)}, s32[256]{0:T(256)}, u32[]{:S(2)}) copy-start(s32[256]{0:T(256)} %new_hbm.7) | copy-start | bytes 3076
  78.5 10.7 %copy-start.8 = (s32[256]{0:T(256)S(1)}, s32[256]{0:T(256)}, u32[]{:S(2)}) copy-start(s32[256]{0:T(256)} %counts_hbm.3) | copy-start | bytes 3076
  78.5 10.7 %copy-start.2 = (f32[96,1024]{1,0:T(8,128)S(1)}, f32[96,1024]{1,0:T(8,128)}, u32[]{:S(2)}) copy-start(f32[96,1024]{1,0:T(8,128)} %copy-done.1) | copy-start | bytes 1179652
  78.5 10.7 %copy-start.4 = (f32[96,1024]{1,0:T(8,128)S(1)}, f32[96,1024]{1,0:T(8,128)}, u32[]{:S(2)}) copy-start(f32[96,1024]{1,0:T(8,128)} %copy-done.3) | copy-start | bytes 1179652
  78.5 10.6 %collective-permute-start.12 = (f32[96,1024]{1,0:T(8,128)S(1)}, f32[96,1024]{1,0:T(8,128)S(1)}, u32[]{:S(2)}, u32[]{:S(2)}) collective-permute-start(f32[96,1024]{1,0:T(8,128)S(1)} %pad_maximum_fusion.2), channel_id=1, source_target_pairs={{0,16},{1,17},{2,18},{3,19},{4,20},{5,21},{6,22},{7,23},{8,24},{9,... | collective-permute-start | bytes 1179656 | tf_op jit(solution)/shard_map/ppermute | solution.py:222
  79.1 12.7 %collective-permute-start.2 = (f32[48,1024]{1,0:T(8,128)S(1)}, f32[48,1024]{1,0:T(8,128)S(1)}, u32[]{:S(2)}, u32[]{:S(2)}) collective-permute-start(f32[48,1024]{1,0:T(8,128)S(1)} %slice.32), channel_id=1, source_target_pairs={{0,16},{1,17},{2,18},{3,19},{4,20},{5,21},{6,22},{7,23},{8,24},{9,... | collective-permute-start | bytes 589832 | tf_op jit(solution)/shard_map/ppermute | solution.py:222
  87.1 4.7 %collective-permute-start.3 = (f32[48,1024]{1,0:T(8,128)S(1)}, f32[48,1024]{1,0:T(8,128)S(1)}, u32[]{:S(2)}, u32[]{:S(2)}) collective-permute-start(f32[48,1024]{1,0:T(8,128)S(1)} %slice.33), channel_id=1, source_target_pairs={{0,16},{1,17},{2,18},{3,19},{4,20},{5,21},{6,22},{7,23},{8,24},{9,... | collective-permute-start | bytes 589832 | tf_op jit(solution)/shard_map/ppermute | solution.py:222

commit v4 on v3

--- a/solution.py
+++ b/solution.py
@@ -13,7 +13,6 @@
 AXES = ("section", "dp")
 PACKS = ((0, 1), (2, 3, 4, 5, 6, 7))
 SWAPS = ((0, 1), (2, 3), (4, 5), (6,), (7,))
-UPDATES = (((0, 1, 2, 3, 4, 5), (0, 1, 2)), ((6, 7), (3, 4)))
 ROUNDS = ((0, 0), (2, 0), (1, 1), (3, 1), (1, 0), (3, 0), (0, 1), (2, 1))
 PARAMS = pltpu.CompilerParams(vmem_limit_bytes=40 * 2**20)
 ALONE = pltpu.CompilerParams(vmem_limit_bytes=62 * 2**20)
@@ -136,11 +135,11 @@
     )
 
 
-def update_kernel(slots, pieces, arrays, earlier, counts_hbm, new_hbm, grads, *refs):
+def update_kernel(slots, pieces, arrays, counts_hbm, new_hbm, grads, *refs):
     held = refs[:arrays]
-    outs = refs[arrays + earlier : arrays + earlier + 4]
-    counts_ref, new_ref, small_sem, out_sem = refs[arrays + earlier + 4 : arrays + earlier + 8]
-    done = refs[arrays + earlier + 8 :]
+    outs = refs[arrays : arrays + 4]
+    counts_ref, new_ref, small_sem, out_sem = refs[arrays + 4 : arrays + 8]
+    done = refs[arrays + 8 :]
     section, rank = lax.axis_index("section"), lax.axis_index("dp")
     small = [
         pltpu.make_async_copy(counts_hbm, counts_ref, small_sem.at[0]),
@@ -176,16 +175,15 @@
         copy.wait()
 
 
-def update(kept, swapped, counts, new_layers, grads, arrived, exchanged, before):
-    slots = 16
+def update(slots, counts, new_layers, grads, arrived, exchanged):
     arrays, pieces = [], []
-    for turn in kept:
+    for turn, got in enumerate(arrived):
         pieces.append((len(arrays), 0, turn, True))
-        arrays.append(arrived[turn])
-    for group in swapped:
-        for number, turn in enumerate(SWAPS[group]):
+        arrays.append(got)
+    for group, got in zip(SWAPS, exchanged):
+        for number, turn in enumerate(group):
             pieces.append((len(arrays), 48 * number, turn, False))
-        arrays.append(exchanged[group])
+        arrays.append(got)
     count = len(pieces)
     hbm = pl.BlockSpec(memory_space=pltpu.HBM)
     vmem = pl.BlockSpec(memory_space=pltpu.VMEM)
@@ -193,19 +191,18 @@
         jax.ShapeDtypeStruct(grads.shape, jnp.bfloat16)
     ]
     return pl.pallas_call(
-        functools.partial(update_kernel, slots, tuple(pieces), len(arrays), len(before)),
+        functools.partial(update_kernel, slots, tuple(pieces), len(arrays)),
         out_shape=shapes,
-        in_specs=[hbm, hbm] + [vmem] * (len(arrays) + 1) + [hbm] * len(before),
+        in_specs=[hbm, hbm] + [vmem] * (len(arrays) + 1),
         out_specs=[hbm] * 4,
         scratch_shapes=[pltpu.SMEM(counts.shape, jnp.int32)] * 2
         + [pltpu.SemaphoreType.DMA((2,)), pltpu.SemaphoreType.DMA((4, count))]
         + [pltpu.VMEM((16 * count, grads.shape[1]), shape.dtype) for shape in shapes],
-        input_output_aliases={len(arrays) + 3 + i: i for i in range(len(before))},
         compiler_params=PARAMS,
         cost_estimate=pl.CostEstimate(
             flops=count * 2**20, bytes_accessed=count * 2**19, transcendentals=count * 2**16
         ),
-    )(counts, new_layers, grads, *arrays, *before)
+    )(counts, new_layers, grads, *arrays)
 
 
 def on_device(master, momentum, variance, grads, counts, old_layers, new_layers):
@@ -222,10 +219,7 @@
         lax.ppermute(jnp.concatenate([arrived[turn][48:] for turn in group]), AXES, SWAP)
         for group in SWAPS
     ]
-    outs = ()
-    for kept, swapped in UPDATES:
-        outs = update(kept, swapped, counts, new_layers, grads, arrived, exchanged, outs)
-    return tuple(outs)
+    return tuple(update(master.shape[0], counts, new_layers, grads, arrived, exchanged))
 
 
 def solution(mesh):

time: 93.9 us -> 93.7 us (level)
  Pallas kernels: 11.6 us -> 10.3 us
  waiting for transfers between devices: 23.8 us -> 24.8 us
    pallas_call x2 -> x1, Pallas kernels: 4.27 us -> 3.02 us  [update(): pl.pallas_call(functools.partial(update_kernel, slots, tuple(pieces), len...]
    ppermute x5, waiting for transfers between devices: 0.01 us -> 1.08 us  [on_device(): lax.ppermute(jnp.concatenate([arrived[turn][48:] for turn in group]), AXE...]
  transfers between devices with their start and end apart: 13 -> 13, of which waited for: 3 -> 4; matrix products, arithmetic and copies ran while one was open for 0% -> 0% of each run, Pallas kernels for 7% -> 4%
where the time goes in v4:
time: 93.7 us; the launch traced here: 93.3 us
  starting transfers between devices  56.9 us (61%)
  waiting for transfers between devices  24.8 us (26%)
  Pallas kernels  10.3 us (11%)
  between operations  1.01 us (1%)
    ppermute x8, starting transfers between devices, on_device(): lax.ppermute(message, AXES, round_pairs(*turn))  48.9 us
    ppermute x8, waiting for transfers between devices, on_device(): lax.ppermute(message, AXES, round_pairs(*turn))  23.8 us
    ppermute x5, starting transfers between devices, on_device(): lax.ppermute(jnp.concatenate([arrived[turn][48:] for turn in group]), AXE...  8.01 us
    pallas_call x2, Pallas kernels, pack(): pl.pallas_call(functools.partial(pack_kernel, slots, rounds), out_shape=[...  7.3 us
    pallas_call x1, Pallas kernels, update(): pl.pallas_call(functools.partial(update_kernel, slots, tuple(pieces), len...  3.02 us
  transfers between devices with their start and end apart: 13, of which 4 were waited for; matrix products, arithmetic and copies ran while one was open for 0% of the time, Pallas kernels for 4%

profile of v4, /device:TPU:89, one launch (start us, length us, event | category | flops | bytes accessed | tf_op | source)
XLA Modules:
  0.0 93.3 jit_solution(6690175243698630469)
XLA Ops:
  0.6 3.2 %shard_map.102 = (f32[96,1024]{1,0:T(8,128)}, f32[96,1024]{1,0:T(8,128)}) custom-call(s32[256]{0:T(256)} %old_hbm.2, s32[256]{0:T(256)} %new_hbm.5, f32[16,16384]{1,0:T(8,128)} %refs_0_.3, f32[16,16384]{1,0:T(8,128)} %refs_1_.3, f32[16,16384]{1,0:T(8,128)} %refs_2_.3), custom_call_target="tpu_custom_call" | custom-call | bytes 3145728 | tf_op jit(solution)/shard_map/pallas_call | solution.py:110
  3.8 2.9 %collective-permute-start.1 = (f32[96,1024]{1,0:T(8,128)}, f32[96,1024]{1,0:T(8,128)S(1)}, u32[]{:S(2)}, u32[]{:S(2)}) collective-permute-start(f32[96,1024]{1,0:T(8,128)} %get-tuple-element.16), channel_id=1, source_target_pairs={{0,128},{1,160},{2,144},{3,176},{4,192},{5,224},{6,208},{7,240},{8... | collective-permute-start | bytes 1179656 | tf_op jit(solution)/shard_map/ppermute | solution.py:216
  6.7 9.4 %collective-permute-start = (f32[96,1024]{1,0:T(8,128)}, f32[96,1024]{1,0:T(8,128)S(1)}, u32[]{:S(2)}, u32[]{:S(2)}) collective-permute-start(f32[96,1024]{1,0:T(8,128)} %get-tuple-element.14), channel_id=1, source_target_pairs={{0,0},{1,32},{2,16},{3,48},{4,64},{5,96},{6,80},{7,112},{8,128},{9... | collective-permute-start | bytes 1179656 | tf_op jit(solution)/shard_map/ppermute | solution.py:216
  16.1 4.1 %shard_map.103 = (f32[96,1024]{1,0:T(8,128)}, f32[96,1024]{1,0:T(8,128)}, f32[96,1024]{1,0:T(8,128)}, f32[96,1024]{1,0:T(8,128)}, f32[96,1024]{1,0:T(8,128)}, /*index=5*/f32[96,1024]{1,0:T(8,128)}) custom-call(s32[256]{0:T(256)} %old_hbm.2, s32[256]{0:T(256)} %new_hbm.5, f32[16,16384]{1,0:T(8,128)} %refs_0_.3, f32[16,16384]{1,0:T(8,128)} %refs_1_.3, ...), custom_call_target="tpu_custom_call" | custom-call | bytes 3145728 | tf_op jit(solution)/shard_map/pallas_call | solution.py:110
  20.2 6.2 %collective-permute-start.2 = (f32[96,1024]{1,0:T(8,128)}, f32[96,1024]{1,0:T(8,128)S(1)}, u32[]{:S(2)}, u32[]{:S(2)}) collective-permute-start(f32[96,1024]{1,0:T(8,128)} %get-tuple-element.18), channel_id=1, source_target_pairs={{0,96},{1,64},{2,112},{3,80},{4,160},{5,128},{6,176},{7,144},{8,22... | collective-permute-start | bytes 1179656 | tf_op jit(solution)/shard_map/ppermute | solution.py:216
  26.4 3.7 %collective-permute-start.3 = (f32[96,1024]{1,0:T(8,128)}, f32[96,1024]{1,0:T(8,128)S(1)}, u32[]{:S(2)}, u32[]{:S(2)}) collective-permute-start(f32[96,1024]{1,0:T(8,128)} %get-tuple-element.19), channel_id=1, source_target_pairs={{0,224},{1,192},{2,240},{3,208},{4,32},{5,0},{6,48},{7,16},{8,96},... | collective-permute-start | bytes 1179656 | tf_op jit(solution)/shard_map/ppermute | solution.py:216
  30.1 6.0 %collective-permute-start.4 = (f32[96,1024]{1,0:T(8,128)}, f32[96,1024]{1,0:T(8,128)S(1)}, u32[]{:S(2)}, u32[]{:S(2)}) collective-permute-start(f32[96,1024]{1,0:T(8,128)} %get-tuple-element.20), channel_id=1, source_target_pairs={{0,64},{1,96},{2,80},{3,112},{4,128},{5,160},{6,144},{7,176},{8,19... | collective-permute-start | bytes 1179656 | tf_op jit(solution)/shard_map/ppermute | solution.py:216
  36.2 0.0 copy-start.1
  36.2 2.1 %collective-permute-start.5 = (f32[96,1024]{1,0:T(8,128)}, f32[96,1024]{1,0:T(8,128)S(1)}, u32[]{:S(2)}, u32[]{:S(2)}) collective-permute-start(f32[96,1024]{1,0:T(8,128)} %get-tuple-element.21), channel_id=1, source_target_pairs={{0,192},{1,224},{2,208},{3,240},{4,0},{5,32},{6,16},{7,48},{8,64},... | collective-permute-start | bytes 1179656 | tf_op jit(solution)/shard_map/ppermute | solution.py:216
  38.3 0.0 copy-start.3
  38.3 6.6 %collective-permute-start.6 = (f32[96,1024]{1,0:T(8,128)S(1)}, f32[96,1024]{1,0:T(8,128)S(1)}, u32[]{:S(2)}, u32[]{:S(2)}) collective-permute-start(f32[96,1024]{1,0:T(8,128)S(1)} %copy-done.10), channel_id=1, source_target_pairs={{0,32},{1,0},{2,48},{3,16},{4,96},{5,64},{6,112},{7,80},{8,160},{9... | collective-permute-start | bytes 1179656 | tf_op jit(solution)/shard_map/ppermute | solution.py:216
  45.0 0.0 copy-start.5
  45.0 0.0 slice-start
  45.0 0.0 slice-start.1
  45.0 12.0 %collective-permute-start.7 = (f32[96,1024]{1,0:T(8,128)S(1)}, f32[96,1024]{1,0:T(8,128)S(1)}, u32[]{:S(2)}, u32[]{:S(2)}) collective-permute-start(f32[96,1024]{1,0:T(8,128)S(1)} %copy-done.9), channel_id=1, source_target_pairs={{0,160},{1,128},{2,176},{3,144},{4,224},{5,192},{6,240},{7,208},{8... | collective-permute-start | bytes 1179656 | tf_op jit(solution)/shard_map/ppermute | solution.py:216
  57.1 0.0 slice-start.2
  57.1 4.1 %collective-permute-done.3.refs_3_ = f32[96,1024]{1,0:T(8,128)S(1)} collective-permute-done((f32[96,1024]{1,0:T(8,128)}, f32[96,1024]{1,0:T(8,128)S(1)}, u32[]{:S(2)}, u32[]{:S(2)}) %collective-permute-start.3) | collective-permute-done | bytes 393248 | tf_op jit(solution)/shard_map/ppermute | solution.py:216
  61.2 0.0 collective-permute-start.8
  61.3 17.1 %collective-permute-done.4.refs_4_ = f32[96,1024]{1,0:T(8,128)S(1)} collective-permute-done((f32[96,1024]{1,0:T(8,128)}, f32[96,1024]{1,0:T(8,128)S(1)}, u32[]{:S(2)}, u32[]{:S(2)}) %collective-permute-start.4) | collective-permute-done | bytes 393248 | tf_op jit(solution)/shard_map/ppermute | solution.py:216
  78.4 0.0 collective-permute-start.9
  78.4 0.0 copy-start
  78.4 0.0 collective-permute-done.5.refs_5_
  78.4 0.0 copy-start.7
  78.5 0.0 copy-start.8
  78.5 0.0 copy-start.2
  78.5 0.0 copy-start.4
  78.5 0.6 collective-permute-start.10
  79.1 5.4 %collective-permute-start.11 = (f32[48,1024]{1,0:T(8,128)S(1)}, f32[48,1024]{1,0:T(8,128)S(1)}, u32[]{:S(2)}, u32[]{:S(2)}) collective-permute-start(f32[48,1024]{1,0:T(8,128)S(1)} %slice.38), channel_id=1, source_target_pairs={{0,16},{1,17},{2,18},{3,19},{4,20},{5,21},{6,22},{7,23},{8,24},{9,... | collective-permute-start | bytes 589832 | tf_op jit(solution)/shard_map/ppermute | solution.py:219
  84.5 2.5 %collective-permute-done.7.refs_7_ = f32[96,1024]{1,0:T(8,128)S(1)} collective-permute-done((f32[96,1024]{1,0:T(8,128)S(1)}, f32[96,1024]{1,0:T(8,128)S(1)}, u32[]{:S(2)}, u32[]{:S(2)}) %collective-permute-start.7) | collective-permute-done | bytes 393248 | tf_op jit(solution)/shard_map/ppermute | solution.py:216
  87.1 2.1 %collective-permute-start.12 = (f32[48,1024]{1,0:T(8,128)S(1)}, f32[48,1024]{1,0:T(8,128)S(1)}, u32[]{:S(2)}, u32[]{:S(2)}) collective-permute-start(f32[48,1024]{1,0:T(8,128)S(1)} %slice.39), channel_id=1, source_target_pairs={{0,16},{1,17},{2,18},{3,19},{4,20},{5,21},{6,22},{7,23},{8,24},{9,... | collective-permute-start | bytes 589832 | tf_op jit(solution)/shard_map/ppermute | solution.py:219
  89.1 1.1 %collective-permute-done.12.refs_12_ = f32[48,1024]{1,0:T(8,128)S(1)} collective-permute-done((f32[48,1024]{1,0:T(8,128)S(1)}, f32[48,1024]{1,0:T(8,128)S(1)}, u32[]{:S(2)}, u32[]{:S(2)}) %collective-permute-start.12) | collective-permute-done | bytes 196640 | tf_op jit(solution)/shard_map/ppermute | solution.py:219
  90.3 3.0 %shard_map.104 = (f32[256,1024]{1,0:T(8,128)}, f32[256,1024]{1,0:T(8,128)}, f32[256,1024]{1,0:T(8,128)}, bf16[256,1024]{1,0:T(8,128)(2,1)}) custom-call(s32[256]{0:T(256)S(1)} %copy-done.8, s32[256]{0:T(256)S(1)} %copy-done.7, f32[256,1024]{1,0:T(8,128)S(1)} %copy-done, f32[96,1024]{1,0:T(8,128)S(1)} %copy-done.4, f32[96,1024]{1,0:T(8,128)S(1)} %copy-done.2, ...), custom_call_target="tpu_custom_call" | custom-call | flops 16777216 | bytes 8388608 | tf_op jit(solution)/shard_map/pallas_call | solution.py:193
  (33 shorter events, 0.2 us)
Async XLA Ops:
  3.8 32.4 %collective-permute-start.1 = (f32[96,1024]{1,0:T(8,128)}, f32[96,1024]{1,0:T(8,128)S(1)}, u32[]{:S(2)}, u32[]{:S(2)}) collective-permute-start(f32[96,1024]{1,0:T(8,128)} %get-tuple-element.16), channel_id=1, source_target_pairs={{0,128},{1,160},{2,144},{3,176},{4,192},{5,224},{6,208},{7,240},{8... | collective-permute-start | bytes 1179656 | tf_op jit(solution)/shard_map/ppermute | solution.py:216
  6.7 31.6 %collective-permute-start = (f32[96,1024]{1,0:T(8,128)}, f32[96,1024]{1,0:T(8,128)S(1)}, u32[]{:S(2)}, u32[]{:S(2)}) collective-permute-start(f32[96,1024]{1,0:T(8,128)} %get-tuple-element.14), channel_id=1, source_target_pairs={{0,0},{1,32},{2,16},{3,48},{4,64},{5,96},{6,80},{7,112},{8,128},{9... | collective-permute-start | bytes 1179656 | tf_op jit(solution)/shard_map/ppermute | solution.py:216
  20.2 18.1 %copy-start.10 = (f32[96,1024]{1,0:T(8,128)S(1)}, f32[96,1024]{1,0:T(8,128)}, u32[]{:S(2)}) copy-start(f32[96,1024]{1,0:T(8,128)} %get-tuple-element.22) | copy-start | bytes 1179652
  20.2 24.7 %collective-permute-start.2 = (f32[96,1024]{1,0:T(8,128)}, f32[96,1024]{1,0:T(8,128)S(1)}, u32[]{:S(2)}, u32[]{:S(2)}) collective-permute-start(f32[96,1024]{1,0:T(8,128)} %get-tuple-element.18), channel_id=1, source_target_pairs={{0,96},{1,64},{2,112},{3,80},{4,160},{5,128},{6,176},{7,144},{8,22... | collective-permute-start | bytes 1179656 | tf_op jit(solution)/shard_map/ppermute | solution.py:216
  26.4 34.8 %collective-permute-start.3 = (f32[96,1024]{1,0:T(8,128)}, f32[96,1024]{1,0:T(8,128)S(1)}, u32[]{:S(2)}, u32[]{:S(2)}) collective-permute-start(f32[96,1024]{1,0:T(8,128)} %get-tuple-element.19), channel_id=1, source_target_pairs={{0,224},{1,192},{2,240},{3,208},{4,32},{5,0},{6,48},{7,16},{8,96},... | collective-permute-start | bytes 1179656 | tf_op jit(solution)/shard_map/ppermute | solution.py:216
  30.1 48.2 %collective-permute-start.4 = (f32[96,1024]{1,0:T(8,128)}, f32[96,1024]{1,0:T(8,128)S(1)}, u32[]{:S(2)}, u32[]{:S(2)}) collective-permute-start(f32[96,1024]{1,0:T(8,128)} %get-tuple-element.20), channel_id=1, source_target_pairs={{0,64},{1,96},{2,80},{3,112},{4,128},{5,160},{6,144},{7,176},{8,19... | collective-permute-start | bytes 1179656 | tf_op jit(solution)/shard_map/ppermute | solution.py:216
  36.2 2.1 %copy-start.1 = (f32[96,1024]{1,0:T(8,128)}, f32[96,1024]{1,0:T(8,128)S(1)}, u32[]{:S(2)}) copy-start(f32[96,1024]{1,0:T(8,128)S(1)} %collective-permute-done.1.refs_1_) | copy-start | bytes 1179652
  36.2 8.8 %copy-start.9 = (f32[96,1024]{1,0:T(8,128)S(1)}, f32[96,1024]{1,0:T(8,128)}, u32[]{:S(2)}) copy-start(f32[96,1024]{1,0:T(8,128)} %get-tuple-element.23) | copy-start | bytes 1179652
  36.2 42.2 %collective-permute-start.5 = (f32[96,1024]{1,0:T(8,128)}, f32[96,1024]{1,0:T(8,128)S(1)}, u32[]{:S(2)}, u32[]{:S(2)}) collective-permute-start(f32[96,1024]{1,0:T(8,128)} %get-tuple-element.21), channel_id=1, source_target_pairs={{0,192},{1,224},{2,208},{3,240},{4,0},{5,32},{6,16},{7,48},{8,64},... | collective-permute-start | bytes 1179656 | tf_op jit(solution)/shard_map/ppermute | solution.py:216
  38.3 6.7 %copy-start.3 = (f32[96,1024]{1,0:T(8,128)}, f32[96,1024]{1,0:T(8,128)S(1)}, u32[]{:S(2)}) copy-start(f32[96,1024]{1,0:T(8,128)S(1)} %collective-permute-done.refs_0_) | copy-start | bytes 1179652
  38.3 40.8 %collective-permute-start.6 = (f32[96,1024]{1,0:T(8,128)S(1)}, f32[96,1024]{1,0:T(8,128)S(1)}, u32[]{:S(2)}, u32[]{:S(2)}) collective-permute-start(f32[96,1024]{1,0:T(8,128)S(1)} %copy-done.10), channel_id=1, source_target_pairs={{0,32},{1,0},{2,48},{3,16},{4,96},{5,64},{6,112},{7,80},{8,160},{9... | collective-permute-start | bytes 1179656 | tf_op jit(solution)/shard_map/ppermute | solution.py:216
  45.0 12.1 %copy-start.5 = (f32[96,1024]{1,0:T(8,128)}, f32[96,1024]{1,0:T(8,128)S(1)}, u32[]{:S(2)}) copy-start(f32[96,1024]{1,0:T(8,128)S(1)} %collective-permute-done.2.refs_2_) | copy-start | bytes 1179652
  45.0 12.0 %slice-start = ((f32[96,1024]{1,0:T(8,128)}), f32[48,1024]{1,0:T(8,128)S(1)}, s32[]{:S(2)}) async-start(f32[96,1024]{1,0:T(8,128)} %copy-done.1), calls=%async_computation | async-start | bytes 393216 | tf_op jit(solution)/shard_map/slice | solution.py:219
  45.0 12.0 %slice-start.1 = ((f32[96,1024]{1,0:T(8,128)}), f32[48,1024]{1,0:T(8,128)S(1)}, s32[]{:S(2)}) async-start(f32[96,1024]{1,0:T(8,128)} %copy-done.3), calls=%async_computation.1 | async-start | bytes 393216 | tf_op jit(solution)/shard_map/slice | solution.py:219
  45.0 42.0 %collective-permute-start.7 = (f32[96,1024]{1,0:T(8,128)S(1)}, f32[96,1024]{1,0:T(8,128)S(1)}, u32[]{:S(2)}, u32[]{:S(2)}) collective-permute-start(f32[96,1024]{1,0:T(8,128)S(1)} %copy-done.9), channel_id=1, source_target_pairs={{0,160},{1,128},{2,176},{3,144},{4,224},{5,192},{6,240},{7,208},{8... | collective-permute-start | bytes 1179656 | tf_op jit(solution)/shard_map/ppermute | solution.py:216
  57.1 4.1 %slice-start.2 = ((f32[96,1024]{1,0:T(8,128)}), f32[48,1024]{1,0:T(8,128)S(1)}, s32[]{:S(2)}) async-start(f32[96,1024]{1,0:T(8,128)} %copy-done.5), calls=%async_computation.2 | async-start | bytes 393216 | tf_op jit(solution)/shard_map/slice | solution.py:219
  61.2 29.0 %collective-permute-start.8 = (f32[96,1024]{1,0:T(8,128)S(1)}, f32[96,1024]{1,0:T(8,128)S(1)}, u32[]{:S(2)}, u32[]{:S(2)}) collective-permute-start(f32[96,1024]{1,0:T(8,128)S(1)} %pad_maximum_fusion), channel_id=1, source_target_pairs={{0,16},{1,17},{2,18},{3,19},{4,20},{5,21},{6,22},{7,23},{8,24},{9,... | collective-permute-start | bytes 1179656 | tf_op jit(solution)/shard_map/ppermute | solution.py:219
  78.4 11.8 %collective-permute-start.9 = (f32[96,1024]{1,0:T(8,128)S(1)}, f32[96,1024]{1,0:T(8,128)S(1)}, u32[]{:S(2)}, u32[]{:S(2)}) collective-permute-start(f32[96,1024]{1,0:T(8,128)S(1)} %pad_maximum_fusion.1), channel_id=1, source_target_pairs={{0,16},{1,17},{2,18},{3,19},{4,20},{5,21},{6,22},{7,23},{8,24},{9,... | collective-permute-start | bytes 1179656 | tf_op jit(solution)/shard_map/ppermute | solution.py:219
  78.4 11.8 %copy-start.6 = (f32[96,1024]{1,0:T(8,128)S(1)}, f32[96,1024]{1,0:T(8,128)}, u32[]{:S(2)}) copy-start(f32[96,1024]{1,0:T(8,128)} %copy-done.5) | copy-start | bytes 1179652
  78.4 11.8 %copy-start = (f32[256,1024]{1,0:T(8,128)S(1)}, f32[256,1024]{1,0:T(8,128)}, u32[]{:S(2)}) copy-start(f32[256,1024]{1,0:T(8,128)} %grads.1) | copy-start | bytes 3145732
  78.4 11.8 %copy-start.7 = (s32[256]{0:T(256)S(1)}, s32[256]{0:T(256)}, u32[]{:S(2)}) copy-start(s32[256]{0:T(256)} %new_hbm.5) | copy-start | bytes 3076
  78.5 11.8 %copy-start.8 = (s32[256]{0:T(256)S(1)}, s32[256]{0:T(256)}, u32[]{:S(2)}) copy-start(s32[256]{0:T(256)} %counts_hbm.1) | copy-start | bytes 3076
  78.5 11.7 %copy-start.2 = (f32[96,1024]{1,0:T(8,128)S(1)}, f32[96,1024]{1,0:T(8,128)}, u32[]{:S(2)}) copy-start(f32[96,1024]{1,0:T(8,128)} %copy-done.1) | copy-start | bytes 1179652
  78.5 11.7 %copy-start.4 = (f32[96,1024]{1,0:T(8,128)S(1)}, f32[96,1024]{1,0:T(8,128)}, u32[]{:S(2)}) copy-start(f32[96,1024]{1,0:T(8,128)} %copy-done.3) | copy-start | bytes 1179652
  78.5 11.7 %collective-permute-start.10 = (f32[96,1024]{1,0:T(8,128)S(1)}, f32[96,1024]{1,0:T(8,128)S(1)}, u32[]{:S(2)}, u32[]{:S(2)}) collective-permute-start(f32[96,1024]{1,0:T(8,128)S(1)} %pad_maximum_fusion.2), channel_id=1, source_target_pairs={{0,16},{1,17},{2,18},{3,19},{4,20},{5,21},{6,22},{7,23},{8,24},{9,... | collective-permute-start | bytes 1179656 | tf_op jit(solution)/shard_map/ppermute | solution.py:219
  79.1 10.0 %collective-permute-start.11 = (f32[48,1024]{1,0:T(8,128)S(1)}, f32[48,1024]{1,0:T(8,128)S(1)}, u32[]{:S(2)}, u32[]{:S(2)}) collective-permute-start(f32[48,1024]{1,0:T(8,128)S(1)} %slice.38), channel_id=1, source_target_pairs={{0,16},{1,17},{2,18},{3,19},{4,20},{5,21},{6,22},{7,23},{8,24},{9,... | collective-permute-start | bytes 589832 | tf_op jit(solution)/shard_map/ppermute | solution.py:219
  87.1 3.1 %collective-permute-start.12 = (f32[48,1024]{1,0:T(8,128)S(1)}, f32[48,1024]{1,0:T(8,128)S(1)}, u32[]{:S(2)}, u32[]{:S(2)}) collective-permute-start(f32[48,1024]{1,0:T(8,128)S(1)} %slice.39), channel_id=1, source_target_pairs={{0,16},{1,17},{2,18},{3,19},{4,20},{5,21},{6,22},{7,23},{8,24},{9,... | collective-permute-start | bytes 589832 | tf_op jit(solution)/shard_map/ppermute | solution.py:219

commit v5 on v3

--- a/solution.py
+++ b/solution.py
@@ -15,6 +15,7 @@
 SWAPS = ((0, 1), (2, 3), (4, 5), (6,), (7,))
 UPDATES = (((0, 1, 2, 3, 4, 5), (0, 1, 2)), ((6, 7), (3, 4)))
 ROUNDS = ((0, 0), (2, 0), (1, 1), (3, 1), (1, 0), (3, 0), (0, 1), (2, 1))
+EARLY = 4
 PARAMS = pltpu.CompilerParams(vmem_limit_bytes=40 * 2**20)
 ALONE = pltpu.CompilerParams(vmem_limit_bytes=62 * 2**20)
 
@@ -123,17 +124,12 @@
     )(old_layers, new_layers, *states)
 
 
-def adamw(weight, first, second, grad, live):
+def adamw(weight, first, second, grad):
     first = 0.9 * first + 0.1 * grad
     second = 0.95 * second + 0.05 * grad * grad
     step_size = first / (1.0 - 0.9**STEP) / (jnp.sqrt(second / (1.0 - 0.95**STEP)) + 1e-08)
     weight = weight - 0.01 * (step_size + 0.1 * weight)
-    zero = jnp.float32(0.0)
-    return (
-        jnp.where(live, weight, zero),
-        jnp.where(live, first, zero),
-        jnp.where(live, second, zero),
-    )
+    return weight, first, second
 
 
 def update_kernel(slots, pieces, arrays, earlier, counts_hbm, new_hbm, grads, *refs):
@@ -148,6 +144,13 @@
     ]
     for copy in small:
         copy.start()
+    for number, (array, offset, turn, kept) in enumerate(pieces[:EARLY]):
+        spot = origin(rank, section, *ROUNDS[turn]) ^ (0 if kept else 2)
+        source = held[array].at[pl.ds(offset, 48)]
+        rows = pl.ds(pl.multiple_of(spot * 16, 16), 16)
+        results = adamw(source[pl.ds(0, 16), :], source[pl.ds(16, 16), :], source[pl.ds(32, 16), :], grads[rows, :])
+        for index, result in enumerate(results):
+            done[index][pl.ds(number * 16, 16), :] = result
     for copy in small:
         copy.wait()
     limit = counts_ref[new_ref[section * slots + rank]]
@@ -161,10 +164,14 @@
         source = held[array].at[pl.ds(offset, 48)]
         rows = pl.ds(pl.multiple_of(spot * 16, 16), 16)
         live = place < limit - spot * (16 * width)
-        results = adamw(
-            source[pl.ds(0, 16), :], source[pl.ds(16, 16), :], source[pl.ds(32, 16), :], grads[rows, :], live
-        )
-        results = (*results, results[0].astype(jnp.bfloat16))
+        if number < EARLY:
+            results = [done[index][pl.ds(number * 16, 16), :] for index in range(3)]
+        else:
+            results = adamw(
+                source[pl.ds(0, 16), :], source[pl.ds(16, 16), :], source[pl.ds(32, 16), :], grads[rows, :]
+            )
+        results = [jnp.where(live, result, jnp.float32(0.0)) for result in results]
+        results.append(results[0].astype(jnp.bfloat16))
         for index, result in enumerate(results):
             done[index][pl.ds(number * 16, 16), :] = result
             copy = pltpu.make_async_copy(

time: 93.9 us -> 93.8 us (level)
  no operation moved by 1% of the time
where the time goes in v5:
time: 93.8 us; the launch traced here: 93.4 us
  starting transfers between devices  56.9 us (61%)
  waiting for transfers between devices  23.8 us (25%)
  Pallas kernels  11.5 us (12%)
  between operations  1.03 us (1%)
    ppermute x8, starting transfers between devices, on_device(): lax.ppermute(message, AXES, round_pairs(*turn))  48.8 us
    ppermute x8, waiting for transfers between devices, on_device(): lax.ppermute(message, AXES, round_pairs(*turn))  23.8 us
    ppermute x5, starting transfers between devices, on_device(): lax.ppermute(jnp.concatenate([arrived[turn][48:] for turn in group]), AXE...  8.04 us
    pallas_call x2, Pallas kernels, pack(): pl.pallas_call(functools.partial(pack_kernel, slots, rounds), out_shape=[...  7.31 us
    pallas_call x2, Pallas kernels, update(): pl.pallas_call(functools.partial(update_kernel, slots, tuple(pieces), len...  4.15 us
  transfers between devices with their start and end apart: 13, of which 3 were waited for; matrix products, arithmetic and copies ran while one was open for 0% of the time, Pallas kernels for 7%

profile of v5, /device:TPU:89, one launch (start us, length us, event | category | flops | bytes accessed | tf_op | source)
XLA Modules:
  0.0 93.4 jit_solution(9772901842258399251)
XLA Ops:
  0.6 3.2 %shard_map.102 = (f32[96,1024]{1,0:T(8,128)}, f32[96,1024]{1,0:T(8,128)}) custom-call(s32[256]{0:T(256)} %old_hbm.2, s32[256]{0:T(256)} %new_hbm.7, f32[16,16384]{1,0:T(8,128)} %refs_0_.3, f32[16,16384]{1,0:T(8,128)} %refs_1_.3, f32[16,16384]{1,0:T(8,128)} %refs_2_.3), custom_call_target="tpu_custom_call" | custom-call | bytes 3145728 | tf_op jit(solution)/shard_map/pallas_call | solution.py:112
  3.8 2.9 %collective-permute-start.5 = (f32[96,1024]{1,0:T(8,128)}, f32[96,1024]{1,0:T(8,128)S(1)}, u32[]{:S(2)}, u32[]{:S(2)}) collective-permute-start(f32[96,1024]{1,0:T(8,128)} %get-tuple-element.23), channel_id=1, source_target_pairs={{0,128},{1,160},{2,144},{3,176},{4,192},{5,224},{6,208},{7,240},{8... | collective-permute-start | bytes 1179656 | tf_op jit(solution)/shard_map/ppermute | solution.py:226
  6.7 9.4 %collective-permute-start.4 = (f32[96,1024]{1,0:T(8,128)}, f32[96,1024]{1,0:T(8,128)S(1)}, u32[]{:S(2)}, u32[]{:S(2)}) collective-permute-start(f32[96,1024]{1,0:T(8,128)} %get-tuple-element.22), channel_id=1, source_target_pairs={{0,0},{1,32},{2,16},{3,48},{4,64},{5,96},{6,80},{7,112},{8,128},{9... | collective-permute-start | bytes 1179656 | tf_op jit(solution)/shard_map/ppermute | solution.py:226
  16.1 4.1 %shard_map.103 = (f32[96,1024]{1,0:T(8,128)}, f32[96,1024]{1,0:T(8,128)}, f32[96,1024]{1,0:T(8,128)}, f32[96,1024]{1,0:T(8,128)}, f32[96,1024]{1,0:T(8,128)}, /*index=5*/f32[96,1024]{1,0:T(8,128)}) custom-call(s32[256]{0:T(256)} %old_hbm.2, s32[256]{0:T(256)} %new_hbm.7, f32[16,16384]{1,0:T(8,128)} %refs_0_.3, f32[16,16384]{1,0:T(8,128)} %refs_1_.3, ...), custom_call_target="tpu_custom_call" | custom-call | bytes 3145728 | tf_op jit(solution)/shard_map/pallas_call | solution.py:112
  20.3 6.2 %collective-permute-start.6 = (f32[96,1024]{1,0:T(8,128)}, f32[96,1024]{1,0:T(8,128)S(1)}, u32[]{:S(2)}, u32[]{:S(2)}) collective-permute-start(f32[96,1024]{1,0:T(8,128)} %get-tuple-element.24), channel_id=1, source_target_pairs={{0,96},{1,64},{2,112},{3,80},{4,160},{5,128},{6,176},{7,144},{8,22... | collective-permute-start | bytes 1179656 | tf_op jit(solution)/shard_map/ppermute | solution.py:226
  26.4 3.7 %collective-permute-start.7 = (f32[96,1024]{1,0:T(8,128)}, f32[96,1024]{1,0:T(8,128)S(1)}, u32[]{:S(2)}, u32[]{:S(2)}) collective-permute-start(f32[96,1024]{1,0:T(8,128)} %get-tuple-element.25), channel_id=1, source_target_pairs={{0,224},{1,192},{2,240},{3,208},{4,32},{5,0},{6,48},{7,16},{8,96},... | collective-permute-start | bytes 1179656 | tf_op jit(solution)/shard_map/ppermute | solution.py:226
  30.1 6.0 %collective-permute-start.8 = (f32[96,1024]{1,0:T(8,128)}, f32[96,1024]{1,0:T(8,128)S(1)}, u32[]{:S(2)}, u32[]{:S(2)}) collective-permute-start(f32[96,1024]{1,0:T(8,128)} %get-tuple-element.26), channel_id=1, source_target_pairs={{0,64},{1,96},{2,80},{3,112},{4,128},{5,160},{6,144},{7,176},{8,19... | collective-permute-start | bytes 1179656 | tf_op jit(solution)/shard_map/ppermute | solution.py:226
  36.2 0.0 collective-permute-done.5.refs_1_
  36.2 2.1 %collective-permute-start.9 = (f32[96,1024]{1,0:T(8,128)}, f32[96,1024]{1,0:T(8,128)S(1)}, u32[]{:S(2)}, u32[]{:S(2)}) collective-permute-start(f32[96,1024]{1,0:T(8,128)} %get-tuple-element.27), channel_id=1, source_target_pairs={{0,192},{1,224},{2,208},{3,240},{4,0},{5,32},{6,16},{7,48},{8,64},... | collective-permute-start | bytes 1179656 | tf_op jit(solution)/shard_map/ppermute | solution.py:226
  38.3 6.6 %collective-permute-start = (f32[96,1024]{1,0:T(8,128)S(1)}, f32[96,1024]{1,0:T(8,128)S(1)}, u32[]{:S(2)}, u32[]{:S(2)}) collective-permute-start(f32[96,1024]{1,0:T(8,128)S(1)} %copy-done.10), channel_id=1, source_target_pairs={{0,32},{1,0},{2,48},{3,16},{4,96},{5,64},{6,112},{7,80},{8,160},{9... | collective-permute-start | bytes 1179656 | tf_op jit(solution)/shard_map/ppermute | solution.py:226
  45.0 0.0 collective-permute-done.6.refs_2_
  45.0 0.0 copy-start.5
  45.0 0.0 slice-start.1
  45.0 12.0 %collective-permute-start.1 = (f32[96,1024]{1,0:T(8,128)S(1)}, f32[96,1024]{1,0:T(8,128)S(1)}, u32[]{:S(2)}, u32[]{:S(2)}) collective-permute-start(f32[96,1024]{1,0:T(8,128)S(1)} %copy-done.9), channel_id=1, source_target_pairs={{0,160},{1,128},{2,176},{3,144},{4,224},{5,192},{6,240},{7,208},{8... | collective-permute-start | bytes 1179656 | tf_op jit(solution)/shard_map/ppermute | solution.py:226
  57.1 0.0 slice-start.2
  57.1 4.1 %collective-permute-done.7.refs_3_ = f32[96,1024]{1,0:T(8,128)S(1)} collective-permute-done((f32[96,1024]{1,0:T(8,128)}, f32[96,1024]{1,0:T(8,128)S(1)}, u32[]{:S(2)}, u32[]{:S(2)}) %collective-permute-start.7) | collective-permute-done | bytes 393248 | tf_op jit(solution)/shard_map/ppermute | solution.py:226
  61.2 0.0 collective-permute-start.10
  61.3 17.1 %collective-permute-done.8.refs_4_ = f32[96,1024]{1,0:T(8,128)S(1)} collective-permute-done((f32[96,1024]{1,0:T(8,128)}, f32[96,1024]{1,0:T(8,128)S(1)}, u32[]{:S(2)}, u32[]{:S(2)}) %collective-permute-start.8) | collective-permute-done | bytes 393248 | tf_op jit(solution)/shard_map/ppermute | solution.py:226
  78.4 0.0 collective-permute-start.11
  78.4 0.0 copy-start
  78.4 0.0 collective-permute-done.9.refs_5_
  78.4 0.0 copy-start.7
  78.5 0.0 copy-start.8
  78.5 0.6 collective-permute-start.12
  79.1 0.0 collective-permute-done.refs_0_
  79.1 5.4 %collective-permute-start.2 = (f32[48,1024]{1,0:T(8,128)S(1)}, f32[48,1024]{1,0:T(8,128)S(1)}, u32[]{:S(2)}, u32[]{:S(2)}) collective-permute-start(f32[48,1024]{1,0:T(8,128)S(1)} %slice.32), channel_id=1, source_target_pairs={{0,16},{1,17},{2,18},{3,19},{4,20},{5,21},{6,22},{7,23},{8,24},{9,... | collective-permute-start | bytes 589832 | tf_op jit(solution)/shard_map/ppermute | solution.py:229
  84.5 2.5 %collective-permute-done.1.refs_1_ = f32[96,1024]{1,0:T(8,128)S(1)} collective-permute-done((f32[96,1024]{1,0:T(8,128)S(1)}, f32[96,1024]{1,0:T(8,128)S(1)}, u32[]{:S(2)}, u32[]{:S(2)}) %collective-permute-start.1) | collective-permute-done | bytes 393248 | tf_op jit(solution)/shard_map/ppermute | solution.py:226
  87.1 2.1 %collective-permute-start.3 = (f32[48,1024]{1,0:T(8,128)S(1)}, f32[48,1024]{1,0:T(8,128)S(1)}, u32[]{:S(2)}, u32[]{:S(2)}) collective-permute-start(f32[48,1024]{1,0:T(8,128)S(1)} %slice.33), channel_id=1, source_target_pairs={{0,16},{1,17},{2,18},{3,19},{4,20},{5,21},{6,22},{7,23},{8,24},{9,... | collective-permute-start | bytes 589832 | tf_op jit(solution)/shard_map/ppermute | solution.py:229
  89.1 0.0 collective-permute-done.10.refs_6_
  89.2 2.5 %shard_map.104 = (f32[256,1024]{1,0:T(8,128)}, f32[256,1024]{1,0:T(8,128)}, f32[256,1024]{1,0:T(8,128)}, bf16[256,1024]{1,0:T(8,128)(2,1)}) custom-call(s32[256]{0:T(256)S(1)} %copy-done.8, s32[256]{0:T(256)S(1)} %copy-done.7, f32[256,1024]{1,0:T(8,128)S(1)} %copy-done, f32[96,1024]{1,0:T(8,128)S(1)} %copy-done.4, f32[96,1024]{1,0:T(8,128)S(1)} %copy-done.2, ...), custom_call_target="tpu_custom_call" | custom-call | flops 12582912 | bytes 6291456 | tf_op jit(solution)/shard_map/pallas_call | solution.py:202
  91.7 0.0 collective-permute-done.2.refs_2_
  91.8 1.6 %shard_map.105 = (f32[256,1024]{1,0:T(8,128)}, f32[256,1024]{1,0:T(8,128)}, f32[256,1024]{1,0:T(8,128)}, bf16[256,1024]{1,0:T(8,128)(2,1)}) custom-call(s32[256]{0:T(256)S(1)} %copy-done.8, s32[256]{0:T(256)S(1)} %copy-done.7, f32[256,1024]{1,0:T(8,128)S(1)} %copy-done, ...), custom_call_target="tpu_custom_call", output_to_operand_aliasing={{0}: (7, {}), {1}: (8, {}), {2}: (9, {}), {3}: (10, {})} | custom-call | flops 4194304 | bytes 2097152 | tf_op jit(solution)/shard_map/pallas_call | solution.py:202
  (34 shorter events, 0.2 us)
Async XLA Ops:
  3.8 32.4 %collective-permute-start.5 = (f32[96,1024]{1,0:T(8,128)}, f32[96,1024]{1,0:T(8,128)S(1)}, u32[]{:S(2)}, u32[]{:S(2)}) collective-permute-start(f32[96,1024]{1,0:T(8,128)} %get-tuple-element.23), channel_id=1, source_target_pairs={{0,128},{1,160},{2,144},{3,176},{4,192},{5,224},{6,208},{7,240},{8... | collective-permute-start | bytes 1179656 | tf_op jit(solution)/shard_map/ppermute | solution.py:226
  6.7 31.6 %collective-permute-start.4 = (f32[96,1024]{1,0:T(8,128)}, f32[96,1024]{1,0:T(8,128)S(1)}, u32[]{:S(2)}, u32[]{:S(2)}) collective-permute-start(f32[96,1024]{1,0:T(8,128)} %get-tuple-element.22), channel_id=1, source_target_pairs={{0,0},{1,32},{2,16},{3,48},{4,64},{5,96},{6,80},{7,112},{8,128},{9... | collective-permute-start | bytes 1179656 | tf_op jit(solution)/shard_map/ppermute | solution.py:226
  20.2 18.1 %copy-start.10 = (f32[96,1024]{1,0:T(8,128)S(1)}, f32[96,1024]{1,0:T(8,128)}, u32[]{:S(2)}) copy-start(f32[96,1024]{1,0:T(8,128)} %get-tuple-element.20) | copy-start | bytes 1179652
  20.3 24.7 %collective-permute-start.6 = (f32[96,1024]{1,0:T(8,128)}, f32[96,1024]{1,0:T(8,128)S(1)}, u32[]{:S(2)}, u32[]{:S(2)}) collective-permute-start(f32[96,1024]{1,0:T(8,128)} %get-tuple-element.24), channel_id=1, source_target_pairs={{0,96},{1,64},{2,112},{3,80},{4,160},{5,128},{6,176},{7,144},{8,22... | collective-permute-start | bytes 1179656 | tf_op jit(solution)/shard_map/ppermute | solution.py:226
  26.4 34.8 %collective-permute-start.7 = (f32[96,1024]{1,0:T(8,128)}, f32[96,1024]{1,0:T(8,128)S(1)}, u32[]{:S(2)}, u32[]{:S(2)}) collective-permute-start(f32[96,1024]{1,0:T(8,128)} %get-tuple-element.25), channel_id=1, source_target_pairs={{0,224},{1,192},{2,240},{3,208},{4,32},{5,0},{6,48},{7,16},{8,96},... | collective-permute-start | bytes 1179656 | tf_op jit(solution)/shard_map/ppermute | solution.py:226
  30.1 48.2 %collective-permute-start.8 = (f32[96,1024]{1,0:T(8,128)}, f32[96,1024]{1,0:T(8,128)S(1)}, u32[]{:S(2)}, u32[]{:S(2)}) collective-permute-start(f32[96,1024]{1,0:T(8,128)} %get-tuple-element.26), channel_id=1, source_target_pairs={{0,64},{1,96},{2,80},{3,112},{4,128},{5,160},{6,144},{7,176},{8,19... | collective-permute-start | bytes 1179656 | tf_op jit(solution)/shard_map/ppermute | solution.py:226
  36.2 2.1 %copy-start.1 = (f32[96,1024]{1,0:T(8,128)}, f32[96,1024]{1,0:T(8,128)S(1)}, u32[]{:S(2)}) copy-start(f32[96,1024]{1,0:T(8,128)S(1)} %collective-permute-done.5.refs_1_) | copy-start | bytes 1179652
  36.2 8.8 %copy-start.9 = (f32[96,1024]{1,0:T(8,128)S(1)}, f32[96,1024]{1,0:T(8,128)}, u32[]{:S(2)}) copy-start(f32[96,1024]{1,0:T(8,128)} %get-tuple-element.21) | copy-start | bytes 1179652
  36.2 42.2 %collective-permute-start.9 = (f32[96,1024]{1,0:T(8,128)}, f32[96,1024]{1,0:T(8,128)S(1)}, u32[]{:S(2)}, u32[]{:S(2)}) collective-permute-start(f32[96,1024]{1,0:T(8,128)} %get-tuple-element.27), channel_id=1, source_target_pairs={{0,192},{1,224},{2,208},{3,240},{4,0},{5,32},{6,16},{7,48},{8,64},... | collective-permute-start | bytes 1179656 | tf_op jit(solution)/shard_map/ppermute | solution.py:226
  38.3 6.7 %copy-start.3 = (f32[96,1024]{1,0:T(8,128)}, f32[96,1024]{1,0:T(8,128)S(1)}, u32[]{:S(2)}) copy-start(f32[96,1024]{1,0:T(8,128)S(1)} %collective-permute-done.4.refs_0_) | copy-start | bytes 1179652
  38.3 40.8 %collective-permute-start = (f32[96,1024]{1,0:T(8,128)S(1)}, f32[96,1024]{1,0:T(8,128)S(1)}, u32[]{:S(2)}, u32[]{:S(2)}) collective-permute-start(f32[96,1024]{1,0:T(8,128)S(1)} %copy-done.10), channel_id=1, source_target_pairs={{0,32},{1,0},{2,48},{3,16},{4,96},{5,64},{6,112},{7,80},{8,160},{9... | collective-permute-start | bytes 1179656 | tf_op jit(solution)/shard_map/ppermute | solution.py:226
  45.0 12.0 %copy-start.5 = (f32[96,1024]{1,0:T(8,128)}, f32[96,1024]{1,0:T(8,128)S(1)}, u32[]{:S(2)}) copy-start(f32[96,1024]{1,0:T(8,128)S(1)} %collective-permute-done.6.refs_2_) | copy-start | bytes 1179652
  45.0 12.0 %slice-start = ((f32[96,1024]{1,0:T(8,128)}), f32[48,1024]{1,0:T(8,128)S(1)}, s32[]{:S(2)}) async-start(f32[96,1024]{1,0:T(8,128)} %copy-done.1), calls=%async_computation | async-start | bytes 393216 | tf_op jit(solution)/shard_map/slice | solution.py:229
  45.0 12.0 %slice-start.1 = ((f32[96,1024]{1,0:T(8,128)}), f32[48,1024]{1,0:T(8,128)S(1)}, s32[]{:S(2)}) async-start(f32[96,1024]{1,0:T(8,128)} %copy-done.3), calls=%async_computation.1 | async-start | bytes 393216 | tf_op jit(solution)/shard_map/slice | solution.py:229
  45.0 42.0 %collective-permute-start.1 = (f32[96,1024]{1,0:T(8,128)S(1)}, f32[96,1024]{1,0:T(8,128)S(1)}, u32[]{:S(2)}, u32[]{:S(2)}) collective-permute-start(f32[96,1024]{1,0:T(8,128)S(1)} %copy-done.9), channel_id=1, source_target_pairs={{0,160},{1,128},{2,176},{3,144},{4,224},{5,192},{6,240},{7,208},{8... | collective-permute-start | bytes 1179656 | tf_op jit(solution)/shard_map/ppermute | solution.py:226
  57.1 4.2 %slice-start.2 = ((f32[96,1024]{1,0:T(8,128)}), f32[48,1024]{1,0:T(8,128)S(1)}, s32[]{:S(2)}) async-start(f32[96,1024]{1,0:T(8,128)} %copy-done.5), calls=%async_computation.2 | async-start | bytes 393216 | tf_op jit(solution)/shard_map/slice | solution.py:229
  61.2 27.9 %collective-permute-start.10 = (f32[96,1024]{1,0:T(8,128)S(1)}, f32[96,1024]{1,0:T(8,128)S(1)}, u32[]{:S(2)}, u32[]{:S(2)}) collective-permute-start(f32[96,1024]{1,0:T(8,128)S(1)} %pad_maximum_fusion), channel_id=1, source_target_pairs={{0,16},{1,17},{2,18},{3,19},{4,20},{5,21},{6,22},{7,23},{8,24},{9,... | collective-permute-start | bytes 1179656 | tf_op jit(solution)/shard_map/ppermute | solution.py:229
  78.4 10.8 %collective-permute-start.11 = (f32[96,1024]{1,0:T(8,128)S(1)}, f32[96,1024]{1,0:T(8,128)S(1)}, u32[]{:S(2)}, u32[]{:S(2)}) collective-permute-start(f32[96,1024]{1,0:T(8,128)S(1)} %pad_maximum_fusion.1), channel_id=1, source_target_pairs={{0,16},{1,17},{2,18},{3,19},{4,20},{5,21},{6,22},{7,23},{8,24},{9,... | collective-permute-start | bytes 1179656 | tf_op jit(solution)/shard_map/ppermute | solution.py:229
  78.4 10.8 %copy-start.6 = (f32[96,1024]{1,0:T(8,128)S(1)}, f32[96,1024]{1,0:T(8,128)}, u32[]{:S(2)}) copy-start(f32[96,1024]{1,0:T(8,128)} %copy-done.5) | copy-start | bytes 1179652
  78.4 10.8 %copy-start = (f32[256,1024]{1,0:T(8,128)S(1)}, f32[256,1024]{1,0:T(8,128)}, u32[]{:S(2)}) copy-start(f32[256,1024]{1,0:T(8,128)} %grads.3) | copy-start | bytes 3145732
  78.4 10.7 %copy-start.7 = (s32[256]{0:T(256)S(1)}, s32[256]{0:T(256)}, u32[]{:S(2)}) copy-start(s32[256]{0:T(256)} %new_hbm.7) | copy-start | bytes 3076
  78.5 10.7 %copy-start.8 = (s32[256]{0:T(256)S(1)}, s32[256]{0:T(256)}, u32[]{:S(2)}) copy-start(s32[256]{0:T(256)} %counts_hbm.3) | copy-start | bytes 3076
  78.5 10.7 %copy-start.2 = (f32[96,1024]{1,0:T(8,128)S(1)}, f32[96,1024]{1,0:T(8,128)}, u32[]{:S(2)}) copy-start(f32[96,1024]{1,0:T(8,128)} %copy-done.1) | copy-start | bytes 1179652
  78.5 10.7 %copy-start.4 = (f32[96,1024]{1,0:T(8,128)S(1)}, f32[96,1024]{1,0:T(8,128)}, u32[]{:S(2)}) copy-start(f32[96,1024]{1,0:T(8,128)} %copy-done.3) | copy-start | bytes 1179652
  78.5 10.6 %collective-permute-start.12 = (f32[96,1024]{1,0:T(8,128)S(1)}, f32[96,1024]{1,0:T(8,128)S(1)}, u32[]{:S(2)}, u32[]{:S(2)}) collective-permute-start(f32[96,1024]{1,0:T(8,128)S(1)} %pad_maximum_fusion.2), channel_id=1, source_target_pairs={{0,16},{1,17},{2,18},{3,19},{4,20},{5,21},{6,22},{7,23},{8,24},{9,... | collective-permute-start | bytes 1179656 | tf_op jit(solution)/shard_map/ppermute | solution.py:229
  79.1 12.6 %collective-permute-start.2 = (f32[48,1024]{1,0:T(8,128)S(1)}, f32[48,1024]{1,0:T(8,128)S(1)}, u32[]{:S(2)}, u32[]{:S(2)}) collective-permute-start(f32[48,1024]{1,0:T(8,128)S(1)} %slice.32), channel_id=1, source_target_pairs={{0,16},{1,17},{2,18},{3,19},{4,20},{5,21},{6,22},{7,23},{8,24},{9,... | collective-permute-start | bytes 589832 | tf_op jit(solution)/shard_map/ppermute | solution.py:229
  87.1 4.7 %collective-permute-start.3 = (f32[48,1024]{1,0:T(8,128)S(1)}, f32[48,1024]{1,0:T(8,128)S(1)}, u32[]{:S(2)}, u32[]{:S(2)}) collective-permute-start(f32[48,1024]{1,0:T(8,128)S(1)} %slice.33), channel_id=1, source_target_pairs={{0,16},{1,17},{2,18},{3,19},{4,20},{5,21},{6,22},{7,23},{8,24},{9,... | collective-permute-start | bytes 589832 | tf_op jit(solution)/shard_map/ppermute | solution.py:229
